TPU v7x, 256 devices: a whole 4x4x8 slice. The times are simulated.
256 devices in a mesh: pairs: 256 (over x, y, z, core).
Axes of the slice: x: 4, y: 4, z: 8, core: 2. Of those that a mesh axis runs over, the one named last changes fastest.
Arguments:
- image_feats: bfloat16 [65536, 768], P('pairs'), may hold values from -6 to 6
- text_feats: bfloat16 [65536, 768], P('pairs'), may hold values from -6 to 6
- image_head: bfloat16 [768, 768], replicated, may hold values from -0.0078125 to 0.0078125
- text_head: bfloat16 [768, 768], replicated, may hold values from -0.0078125 to 0.0078125
- logit_scale: float32 [1], replicated, may hold values from 4 to 16
- logit_bias: float32 [1], replicated, may hold values from -6 to -2
- round_offsets: int32 [4], replicated, may hold values from 1 to 255, as said below
Outputs:
- image_grad: bfloat16 [65536, 768], P('pairs')
- text_grad: bfloat16 [65536, 768], P('pairs')
- image_head_grad: float32 [768, 768], replicated
- text_head_grad: float32 [768, 768], replicated
- scalar_grads: float32 [3], replicated
Inputs may be any that keep to these rules, and one draw needn't show every extreme that they name: `round_offsets`: the 4 offsets are distinct; 1 and 256 - 1 are among them.
All inputs are finite; a program needn't handle non-finite values.
Results may differ from a plain program's by a relative error of at most 0.0065.
Values may be sent and summed in bfloat16 or wider, within the bound.
No kernel may reach another device: no remote copies, remote signals or barrier semaphores. Data moves between devices by JAX's collectives and lax.ppermute only.
A program may use at most 128 MiB of HBM per device.

v0:
```python
import jax
import jax.numpy as jnp
from jax import lax
from jax.experimental import pallas as pl
from jax.experimental.pallas import tpu as pltpu
from jax.sharding import PartitionSpec as P

EPS = 1e-06
X, Y, Z, CORES = 4, 4, 8, 2
COUNT = X * Y * Z * CORES
STEP = Z * CORES
SPREAD = X * Y

PLANES = [[xy * STEP + zc for xy in range(X * Y)] for zc in range(STEP)]
COLUMNS = [[xy * STEP + z * CORES + c for z in range(Z)] for xy in range(X * Y) for c in range(CORES)]


def shifted(value, steps):
    return lax.ppermute(value, "pairs", [(source, (source + steps) % COUNT) for source in range(COUNT)])


def other_core(value):
    return lax.ppermute(value, "pairs", [(source, source ^ 1) for source in range(COUNT)])


def exchange(value, groups):
    return lax.all_to_all(value, "pairs", 0, 0, axis_index_groups=groups, tiled=True)


def embed_kernel(xi_hbm, xt_hbm, wi_hbm, wt_hbm, both_ref, u_ref, x_ref, w_ref, sems):
    rows, width = xi_hbm.shape
    piece = both_ref.shape[1] // 2
    copies = []
    for k, (x_hbm, w_hbm) in enumerate(((xi_hbm, wi_hbm), (xt_hbm, wt_hbm))):
        copies.append(pltpu.make_async_copy(x_hbm, x_ref.at[k], sems.at[k, 0]))
        copies.append(pltpu.make_async_copy(w_hbm, w_ref.at[k], sems.at[k, 1]))
    for copy in copies:
        copy.start()
    for k in range(2):
        copies[2 * k].wait()
        copies[2 * k + 1].wait()
        proj = jnp.dot(x_ref[k], w_ref[k], preferred_element_type=jnp.float32)
        norms = jnp.sqrt(jnp.sum(proj * proj, axis=-1, keepdims=True) + EPS)
        z = (proj / norms).astype(jnp.bfloat16)
        u_ref[k * rows : (k + 1) * rows, :] = proj
        both_ref[:, k * piece : (k + 1) * piece, :] = z.reshape(SPREAD, piece, width)


def embed(image_feats, text_feats, image_head, text_head):
    rows, width = image_feats.shape
    vmem = pl.BlockSpec(memory_space=pltpu.VMEM)
    return pl.pallas_call(
        embed_kernel,
        out_shape=(
            jax.ShapeDtypeStruct((SPREAD, 2 * rows // SPREAD, width), jnp.bfloat16),
            jax.ShapeDtypeStruct((2 * rows, width), jnp.float32),
        ),
        in_specs=[pl.BlockSpec(memory_space=pl.ANY)] * 4,
        out_specs=(vmem,) * 2,
        scratch_shapes=[
            pltpu.VMEM((2, rows, width), jnp.bfloat16),
            pltpu.VMEM((2, width, width), jnp.bfloat16),
            pltpu.SemaphoreType.DMA((2, 2)),
        ],
        compiler_params=pltpu.CompilerParams(vmem_limit_bytes=60 * 1024 * 1024),
        name="embed",
    )(image_feats, text_feats, image_head, text_head)


def turned(value, steps):
    pairs = [(source, source // STEP * STEP + (source + steps) % STEP) for source in range(COUNT)]
    return lax.ppermute(value, "pairs", pairs)


def along(txt, img, low):
    def branch(steps):
        if steps == 0:
            return lambda txt, img: (txt, img)
        return lambda txt, img: (turned(txt, -steps), turned(img, steps))

    return tuple(lax.switch(low, [branch(k) for k in range(STEP)], txt, img))


def line_up_kernel(at_ref, a_ref, b_ref, c_ref, d_ref, out_ref):
    piece = a_ref.shape[1]
    for k, ref in enumerate((a_ref, b_ref, c_ref, d_ref)):
        for p in range(SPREAD):
            out_ref[p, k * piece : (k + 1) * piece, :] = ref[lax.rem(at_ref[k] + p, SPREAD)]


def line_up(at, parts):
    vmem = pl.BlockSpec(memory_space=pltpu.VMEM)
    slots, piece, width = parts[0].shape
    return pl.pallas_call(
        line_up_kernel,
        out_shape=jax.ShapeDtypeStruct((slots, len(parts) * piece, width), parts[0].dtype),
        in_specs=[pl.BlockSpec(memory_space=pltpu.SMEM)] + [vmem] * len(parts),
        out_specs=vmem,
        compiler_params=pltpu.CompilerParams(vmem_limit_bytes=16 * 1024 * 1024),
        name="line_up",
    )(at, *parts)


def fetch(both, offsets):
    piece = both.shape[1] // 2
    place = lax.axis_index("pairs") % STEP
    spread, ahead, behind = lax.optimization_barrier((exchange(both, PLANES), shifted(both, -1), shifted(both, 1)))
    img, txt = spread[:, :piece], spread[:, piece:]

    def turns(low):
        return jnp.minimum(jnp.mod(low, STEP), jnp.mod(-low, STEP))

    swap = turns(offsets[0]) > turns(offsets[1])
    one = jnp.where(swap, offsets[1], offsets[0])
    two = jnp.where(swap, offsets[0], offsets[1])
    one_txt, one_img = along(txt, img, jnp.mod(one, STEP))
    chain = turns(two - one) < turns(two)
    two_txt, two_img = along(
        jnp.where(chain, one_txt, txt),
        jnp.where(chain, one_img, img),
        jnp.mod(jnp.where(chain, two - one, two), STEP),
    )
    at = []
    for offset in (one, two):
        low, high = offset % STEP, offset // STEP
        at += [jnp.mod(high + (place + low) // STEP, SPREAD), jnp.mod(SPREAD - high - (place < low), SPREAD)]
    far = line_up(jnp.stack(at).astype(jnp.int32), (one_txt, one_img, two_txt, two_img))
    return ahead, behind, exchange(far, PLANES)


def dot_t(left, right):
    return lax.dot_general(left, right, (((1,), (1,)), ((), ())), preferred_element_type=jnp.float32)


def piece_of(ref, k, count=2):
    slots, rows, width = ref.shape
    rows = rows // count
    return ref[:, k * rows : (k + 1) * rows, :].reshape(slots * rows, width)


def fold(x):
    return jnp.sum(x.reshape(x.shape[0] // 8, 8, x.shape[1]), axis=0)


def gate(sb_ref, cosine, own):
    logit = sb_ref[0] * cosine + sb_ref[1]
    v = logit if own is None else jnp.where(own, -logit, logit)
    e = jnp.exp(-jnp.abs(v))
    inv = 1.0 / (1.0 + e)
    dlogit = jnp.where(v >= 0, inv, e * inv)
    if own is not None:
        dlogit = jnp.where(own, -dlogit, dlogit)
    return jnp.maximum(v, 0.0) + jnp.log1p(e), dlogit


def tile_pair(sb_ref, zi, zt, txt, img, own=None):
    cosine = dot_t(zi, txt)
    loss, dlogit = gate(sb_ref, cosine, own)
    coef = (sb_ref[0] * dlogit).astype(jnp.bfloat16)
    if own is None:
        coef_back = (sb_ref[0] * gate(sb_ref, dot_t(zt, img), None)[1]).astype(jnp.bfloat16)
    else:
        coef_back = coef.T
    to_img = jnp.dot(coef, txt, preferred_element_type=jnp.float32)
    to_txt = jnp.dot(coef_back, img, preferred_element_type=jnp.float32)
    return to_img, to_txt, fold(loss), fold(dlogit * cosine), fold(dlogit)


def added(left, right):
    return [a + b for a, b in zip(left, right)]


def near_kernel(sb_ref, both_ref, ahead_ref, behind_ref, dz_ref, stats_ref):
    zi, zt = piece_of(both_ref, 0), piece_of(both_ref, 1)
    rows = zi.shape[0]
    own = lax.broadcasted_iota(jnp.int32, (rows, rows), 0) == lax.broadcasted_iota(jnp.int32, (rows, rows), 1)
    sums = tile_pair(sb_ref, zi, zt, zt, zi, own)
    sums = added(sums, tile_pair(sb_ref, zi, zt, piece_of(ahead_ref, 1), piece_of(behind_ref, 0)))
    sums = added(sums, tile_pair(sb_ref, zi, zt, piece_of(behind_ref, 1), piece_of(ahead_ref, 0)))
    for k in range(2):
        dz_ref[k] = sums[k]
    for k in range(3):
        stats_ref[k] = sums[2 + k]


def near(sb, *arrays):
    slots, rows, width = arrays[0].shape
    rows = slots * rows // 2
    vmem = pl.BlockSpec(memory_space=pltpu.VMEM)
    return pl.pallas_call(
        near_kernel,
        out_shape=(
            jax.ShapeDtypeStruct((2, rows, width), jnp.float32),
            jax.ShapeDtypeStruct((3, 8, rows), jnp.float32),
        ),
        in_specs=[pl.BlockSpec(memory_space=pltpu.SMEM)] + [vmem] * len(arrays),
        out_specs=(vmem, vmem),
        compiler_params=pltpu.CompilerParams(vmem_limit_bytes=32 * 1024 * 1024),
        cost_estimate=pl.CostEstimate(flops=30 * rows * rows * width, bytes_accessed=8 * rows * width * 2, transcendentals=0),
        name="near",
    )(sb, *arrays)


def last_kernel(sb_ref, core_ref, both_ref, far_ref, dz_ref, stats_ref, u_hbm, xi_hbm, xt_hbm,
                dui_ref, dut_ref, kept_ref, given_ref, u_ref, x_ref, sems):
    copies = [
        pltpu.make_async_copy(u_hbm, u_ref, sems.at[0]),
        pltpu.make_async_copy(xi_hbm, x_ref.at[0], sems.at[1]),
        pltpu.make_async_copy(xt_hbm, x_ref.at[1], sems.at[2]),
    ]
    for copy in copies:
        copy.start()
    zi, zt = piece_of(both_ref, 0), piece_of(both_ref, 1)
    rows, width = zi.shape
    sums = tile_pair(sb_ref, zi, zt, piece_of(far_ref, 0, 4), piece_of(far_ref, 1, 4))
    sums = added(sums, tile_pair(sb_ref, zi, zt, piece_of(far_ref, 2, 4), piece_of(far_ref, 3, 4)))
    copies[0].wait()
    for k, du_ref in enumerate((dui_ref, dut_ref)):
        dz = dz_ref[k] + sums[k]
        proj = u_ref[k * rows : (k + 1) * rows, :]
        norms = jnp.sqrt(jnp.sum(proj * proj, axis=-1, keepdims=True) + EPS)
        zh = proj / norms
        inner = jnp.sum(zh * dz, axis=-1, keepdims=True)
        du_ref[...] = ((dz - zh * inner) / norms).astype(jnp.bfloat16)
    copies[1].wait()
    copies[2].wait()

    def head_grad(out_ref, x, du_ref):
        out_ref[0:width, :] = lax.dot_general(
            x, du_ref[...], (((0,), (0,)), ((), ())), preferred_element_type=jnp.float32
        ).astype(out_ref.dtype)

    core = core_ref[0]

    @pl.when(core == 0)
    def _():
        head_grad(given_ref, x_ref[1], dut_ref)
        head_grad(kept_ref, x_ref[0], dui_ref)

    @pl.when(core == 1)
    def _():
        head_grad(given_ref, x_ref[0], dui_ref)
        head_grad(kept_ref, x_ref[1], dut_ref)

    loss, gscale, gbias = (jnp.sum(stats_ref[k] + sums[2 + k]) for k in range(3))
    row = lax.broadcasted_iota(jnp.int32, (16, width), 0)
    at = lax.broadcasted_iota(jnp.int32, (16, width), 1)
    stats = jnp.where(at == 0, loss, jnp.where(at == 1, gscale, gbias))
    stats = jnp.where(at < 3, stats, 0.0)
    kept_ref[width : width + 8, :] = stats[0:8]
    one = stats.astype(jnp.bfloat16).astype(jnp.float32)
    two = (stats - one).astype(jnp.bfloat16).astype(jnp.float32)
    terms = jnp.where(row == 0, one, jnp.where(row == 1, two, jnp.where(row == 2, stats - one - two, 0.0)))
    given_ref[width : width + 16, :] = terms.astype(jnp.bfloat16)


def last(sb, core, both, far, dz, stats, u, image_feats, text_feats):
    rows, width = image_feats.shape
    vmem = pl.BlockSpec(memory_space=pltpu.VMEM)
    return pl.pallas_call(
        last_kernel,
        out_shape=(
            jax.ShapeDtypeStruct((rows, width), jnp.bfloat16),
            jax.ShapeDtypeStruct((rows, width), jnp.bfloat16),
            jax.ShapeDtypeStruct((width + 8, width), jnp.float32),
            jax.ShapeDtypeStruct((width + 16, width), jnp.bfloat16),
        ),
        in_specs=[pl.BlockSpec(memory_space=pltpu.SMEM)] * 2 + [vmem] * 4 + [pl.BlockSpec(memory_space=pl.ANY)] * 3,
        out_specs=(vmem,) * 4,
        scratch_shapes=[
            pltpu.VMEM((2 * rows, width), jnp.float32),
            pltpu.VMEM((2, rows, width), jnp.bfloat16),
            pltpu.SemaphoreType.DMA((3,)),
        ],
        compiler_params=pltpu.CompilerParams(vmem_limit_bytes=40 * 1024 * 1024),
        name="last",
    )(sb, core, both, far, dz, stats, u, image_feats, text_feats)


def summed_heads(given, kept, total):
    width = kept.shape[1]
    rows = width // (X * Y)
    got = other_core(given).astype(jnp.float32)
    part = (kept[:width] + got[:width]).astype(jnp.bfloat16)
    stats = kept[width, 0:3] + jnp.sum(got[width : width + 3, 0:3], axis=0)
    one = lax.reduce_precision(stats, 8, 7)
    two = lax.reduce_precision(stats - one, 8, 7)
    three = stats - one - two
    terms = jnp.stack([one, two, three])
    extra = jnp.zeros((8, width), jnp.bfloat16).at[0:3, 0:3].set(terms.astype(jnp.bfloat16))
    plane = jnp.concatenate([part.reshape(X * Y, rows, width), jnp.broadcast_to(extra[None], (X * Y, 8, width))], axis=1)
    plane = exchange(plane, PLANES)
    plane = jnp.sum(plane.astype(jnp.float32), axis=0)
    stats = jnp.sum(plane[rows : rows + 3, 0:3], axis=0)
    few = rows // Z
    extra = jnp.zeros((8 - few, width), jnp.float32).at[0, 0:3].set(stats)
    column = jnp.concatenate([plane[:rows].reshape(Z, few, width), jnp.broadcast_to(extra[None], (Z, 8 - few, width))], axis=1)
    column = jnp.sum(exchange(column, COLUMNS), axis=0) / total
    stats = column[few, 0:3]
    part = column[:few].astype(jnp.bfloat16)
    part = exchange(jnp.broadcast_to(part[None], (Z, few, width)), COLUMNS).reshape(rows, width)
    part = exchange(jnp.broadcast_to(part[None], (X * Y, rows, width)), PLANES).reshape(width, width)
    return part, stats


def local(image_feats, text_feats, image_head, text_head, logit_scale, logit_bias, round_offsets):
    total = float(COUNT * image_feats.shape[0])
    both, u = embed(image_feats, text_feats, image_head, text_head)
    order = jnp.sort(round_offsets)
    ahead, behind, far = fetch(both, (order[1], order[2]))
    sb = jnp.concatenate([logit_scale, logit_bias])
    core = lax.axis_index("pairs") % CORES
    dz, stats = near(sb, both, ahead, behind)
    du_img, du_txt, kept, given = last(sb, core.reshape(1), both, far, dz, stats, u, image_feats, text_feats)
    part, sum_stats = summed_heads(given, kept, total)
    first = core == 0
    theirs = other_core(part)
    sum_wi = jnp.where(first, part, theirs).astype(jnp.float32)
    sum_wt = jnp.where(first, theirs, part).astype(jnp.float32)

    g_img = jnp.dot(du_img, image_head.T, preferred_element_type=jnp.float32).astype(jnp.bfloat16)
    g_txt = jnp.dot(du_txt, text_head.T, preferred_element_type=jnp.float32).astype(jnp.bfloat16)
    return (g_img, g_txt, sum_wi, sum_wt, sum_stats)


def solution(mesh):
    placed = (P("pairs", None), P("pairs", None), P(), P(), P(), P(), P())
    return jax.shard_map(
        local,
        mesh=mesh,
        in_specs=placed,
        out_specs=(P("pairs", None), P("pairs", None), P(), P(), P()),
        check_vma=False,
    )
```

profile of v0, /device:TPU:1, one launch (start us, length us, event | category | flops | bytes accessed | tf_op | source)
XLA Modules:
  0.0 218.7 jit_solution(14612332510360076070)
XLA Ops:
  0.6 4.1 %embed.1 = (bf16[16,32,768]{2,1,0:T(8,128)(2,1)}, f32[512,768]{1,0:T(8,128)}) custom-call(bf16[256,768]{1,0:T(8,128)(2,1)} %xi_hbm.3, bf16[256,768]{1,0:T(8,128)(2,1)} %xt_hbm.3, bf16[768,768]{1,0:T(8,128)(2,1)} %wi_hbm.1, bf16[768,768]{1,0:T(8,128)(2,1)} %wt_hbm.1), custom_call_target="tpu_custom_call" | custom-call | tf_op jit(solution)/shard_map/embed/pallas_call | solution.py:52
  4.8 3.3 %collective-permute-start.60 = (bf16[16,32,768]{2,1,0:T(8,128)(2,1)}, bf16[16,32,768]{2,1,0:T(8,128)(2,1)S(1)}, u32[]{:S(2)}, u32[]{:S(2)}) collective-permute-start(bf16[16,32,768]{2,1,0:T(8,128)(2,1)} %get-tuple-element.234.both_ref), channel_id=1, source_target_pairs={{0,255},{1,0},{2,1},{3,2},{4,3},{5,4},{6,5},{7,6},{8,7},{9,8},{10,... | collective-permute-start | bytes 2359304 | tf_op jit(solution)/shard_map/ppermute | solution.py:19
  8.1 6.6 %all-to-all-start = ((bf16[16,32,768]{2,1,0:T(8,128)(2,1)}), bf16[16,32,768]{2,1,0:T(8,128)(2,1)S(1)}, u32[]{:S(2)}, u32[]{:S(2)}) async-start(bf16[16,32,768]{2,1,0:T(8,128)(2,1)} %get-tuple-element.234.both_ref), calls=%async_computation | async-start | bytes 1572864 | tf_op jit(solution)/shard_map/all_to_all | solution.py:27
  24.3 11.5 %all-to-all-done = bf16[16,32,768]{2,1,0:T(8,128)(2,1)S(1)} async-done(((bf16[16,32,768]{2,1,0:T(8,128)(2,1)}), bf16[16,32,768]{2,1,0:T(8,128)(2,1)S(1)}, u32[]{:S(2)}, u32[]{:S(2)}) %all-to-all-start) | async-done | bytes 786464 | tf_op jit(solution)/shard_map/all_to_all | solution.py:27
  36.9 28.8 %conditional.2 = ((bf16[16,16,768]{2,1,0:T(8,128)(2,1)S(1)}, bf16[16,16,768]{2,1,0:T(8,128)(2,1)S(1)})) conditional(s32[]{:T(128)} %clamp.6, (bf16[16,16,768]{2,1,0:T(8,128)(2,1)S(1)}, bf16[16,16,768]{2,1,0:T(8,128)(2,1)S(1)}) %tuple.144, (bf16[16,16,768]{2,1,0:T(8,128)(2,1)S(1)}, ...), branch_computations={%region_1.2_spmd, %region_2.3_spmd, %region_3.4_spmd, %region_4.5_... | conditional | bytes 4718696 | solution.py:81
  50.6 2.9 %collective-permute-start.25 = (bf16[16,16,768]{2,1,0:T(8,128)(2,1)S(1)}, bf16[16,16,768]{2,1,0:T(8,128)(2,1)S(1)}, u32[]{:S(2)}, u32[]{:S(2)}) collective-permute-start(bf16[16,16,768]{2,1,0:T(8,128)(2,1)S(1)} %get-tuple-element.178), channel_id=1, source_target_pairs={{0,13},{1,14},{2,15},{3,0},{4,1},{5,2},{6,3},{7,4},{8,5},{9,6},{10... | collective-permute-start | bytes 1179656 | tf_op jit(solution)/shard_map/cond/branch_13_fun/ppermute | solution.py:72
  53.5 9.5 %collective-permute-done.24 = bf16[16,16,768]{2,1,0:T(8,128)(2,1)S(1)} collective-permute-done((bf16[16,16,768]{2,1,0:T(8,128)(2,1)S(1)}, bf16[16,16,768]{2,1,0:T(8,128)(2,1)S(1)}, u32[]{:S(2)}, u32[]{:S(2)}) %collective-permute-start.24) | collective-permute-done | bytes 393248 | tf_op jit(solution)/shard_map/cond/branch_13_fun/ppermute | solution.py:72
  63.1 2.6 %collective-permute-done.25 = bf16[16,16,768]{2,1,0:T(8,128)(2,1)S(1)} collective-permute-done((bf16[16,16,768]{2,1,0:T(8,128)(2,1)S(1)}, bf16[16,16,768]{2,1,0:T(8,128)(2,1)S(1)}, u32[]{:S(2)}, u32[]{:S(2)}) %collective-permute-start.25) | collective-permute-done | bytes 393248 | tf_op jit(solution)/shard_map/cond/branch_13_fun/ppermute | solution.py:72
  65.8 32.0 %conditional.3 = ((bf16[16,16,768]{2,1,0:T(8,128)(2,1)S(1)}, bf16[16,16,768]{2,1,0:T(8,128)(2,1)S(1)})) conditional(s32[]{:T(128)} %clamp.7, (bf16[16,16,768]{2,1,0:T(8,128)(2,1)S(1)}, bf16[16,16,768]{2,1,0:T(8,128)(2,1)S(1)}) %tuple.145, (bf16[16,16,768]{2,1,0:T(8,128)(2,1)S(1)}, ...), branch_computations={%region_17.18_spmd, %region_18.19_spmd, %region_19.20_spmd, %regio... | conditional | bytes 4718696 | solution.py:81
  66.2 2.5 %collective-permute-start.48 = (bf16[16,16,768]{2,1,0:T(8,128)(2,1)S(1)}, bf16[16,16,768]{2,1,0:T(8,128)(2,1)S(1)}, u32[]{:S(2)}, u32[]{:S(2)}) collective-permute-start(bf16[16,16,768]{2,1,0:T(8,128)(2,1)S(1)} %get-tuple-element.201), channel_id=1, source_target_pairs={{0,6},{1,7},{2,8},{3,9},{4,10},{5,11},{6,12},{7,13},{8,14},{9,15},... | collective-permute-start | bytes 1179656 | tf_op jit(solution)/shard_map/cond/branch_10_fun/ppermute | solution.py:72
  68.8 2.0 collective-permute-start.49
  70.8 23.1 %collective-permute-done.48 = bf16[16,16,768]{2,1,0:T(8,128)(2,1)S(1)} collective-permute-done((bf16[16,16,768]{2,1,0:T(8,128)(2,1)S(1)}, bf16[16,16,768]{2,1,0:T(8,128)(2,1)S(1)}, u32[]{:S(2)}, u32[]{:S(2)}) %collective-permute-start.48) | collective-permute-done | bytes 393248 | tf_op jit(solution)/shard_map/cond/branch_10_fun/ppermute | solution.py:72
  94.0 3.8 %collective-permute-done.49 = bf16[16,16,768]{2,1,0:T(8,128)(2,1)S(1)} collective-permute-done((bf16[16,16,768]{2,1,0:T(8,128)(2,1)S(1)}, bf16[16,16,768]{2,1,0:T(8,128)(2,1)S(1)}, u32[]{:S(2)}, u32[]{:S(2)}) %collective-permute-start.49) | collective-permute-done | bytes 393248 | tf_op jit(solution)/shard_map/cond/branch_10_fun/ppermute | solution.py:72
  97.8 1.8 line_up.1
  99.7 6.3 %all-to-all-start.1 = ((bf16[16,64,768]{2,1,0:T(8,128)(2,1)}), bf16[16,64,768]{2,1,0:T(8,128)(2,1)S(1)}, u32[]{:S(2)}, u32[]{:S(2)}) async-start(bf16[16,64,768]{2,1,0:T(8,128)(2,1)} %line_up.1), calls=%async_computation.1 | async-start | bytes 3145728 | tf_op jit(solution)/shard_map/all_to_all | solution.py:27
  107.3 1.1 copy-done.11
  109.6 2.5 %near.1 = (f32[2,256,768]{2,1,0:T(8,128)S(1)}, f32[3,8,256]{2,1,0:T(8,128)S(1)}) custom-call(f32[2]{0:T(128)S(1)} %pad_maximum_fusion.2.sb_ref, bf16[16,32,768]{2,1,0:T(8,128)(2,1)S(1)} %copy-done, bf16[16,32,768]{2,1,0:T(8,128)(2,1)S(1)} %copy-done.11, bf16[16,32,768]{2,1,0:T(8,128)(2,1)S(1)} %copy-done.13), custom_call_target="tpu_custom_call" | custom-call | flops 1509949440 | bytes 3145728 | tf_op jit(solution)/shard_map/near/pallas_call | solution.py:190
  112.2 1.2 copy-done.2
  113.9 14.0 %all-to-all-done.1.far_ref = bf16[16,64,768]{2,1,0:T(8,128)(2,1)S(1)} async-done(((bf16[16,64,768]{2,1,0:T(8,128)(2,1)}), bf16[16,64,768]{2,1,0:T(8,128)(2,1)S(1)}, u32[]{:S(2)}, u32[]{:S(2)}) %all-to-all-start.1) | async-done | bytes 1572896 | tf_op jit(solution)/shard_map/all_to_all | solution.py:27
  128.0 1.4 copy-done.1
  129.4 1.4 copy-done.3
  131.5 4.2 %last.1 = (bf16[256,768]{1,0:T(8,128)(2,1)S(1)}, bf16[256,768]{1,0:T(8,128)(2,1)S(1)}, f32[776,768]{1,0:T(8,128)S(1)}, bf16[784,768]{1,0:T(8,128)(2,1)S(1)}) custom-call(f32[2]{0:T(128)S(1)} %pad_maximum_fusion.2.sb_ref, s32[1]{0:T(128)} %bitcast.core_ref, bf16[16,32,768]{2,1,0:T(8,128)(2,1)S(1)} %copy-done, ...), custom_call_target="tpu_custom_call" | custom-call | tf_op jit(solution)/shard_map/last/pallas_call | solution.py:260
  135.7 3.0 %collective-permute-start.62 = (bf16[784,768]{1,0:T(8,128)(2,1)S(1)}, bf16[784,768]{1,0:T(8,128)(2,1)S(1)}, u32[]{:S(2)}, u32[]{:S(2)}) collective-permute-start(bf16[784,768]{1,0:T(8,128)(2,1)S(1)} %get-tuple-element.249), channel_id=1, source_target_pairs={{0,1},{1,0},{2,3},{3,2},{4,5},{5,4},{6,7},{7,6},{8,9},{9,8},{10,11... | collective-permute-start | bytes 3612680 | tf_op jit(solution)/shard_map/ppermute | solution.py:23
  138.8 2.5 %collective-permute-done.62 = bf16[784,768]{1,0:T(8,128)(2,1)S(1)} collective-permute-done((bf16[784,768]{1,0:T(8,128)(2,1)S(1)}, bf16[784,768]{1,0:T(8,128)(2,1)S(1)}, u32[]{:S(2)}, u32[]{:S(2)}) %collective-permute-start.62) | collective-permute-done | bytes 1204256 | tf_op jit(solution)/shard_map/ppermute | solution.py:23
  142.2 22.5 %all_to_all.30 = bf16[16,56,768]{2,1,0:T(8,128)(2,1)S(1)} all-to-all(bf16[16,56,768]{2,1,0:T(8,128)(2,1)S(1)} %pad_maximum_fusion), channel_id=1, replica_groups={{0,16,32,48,64,80,96,112,128,144,160,176,192,208,224,240},{1,17,33,49,6..., dimensions={0} | all-to-all | bytes 2752512 | tf_op jit(solution)/shard_map/all_to_all | solution.py:27
  165.0 12.9 %all_to_all.31 = f32[8,8,768]{2,1,0:T(8,128)S(1)} all-to-all(f32[8,8,768]{2,1,0:T(8,128)S(1)} %pad_maximum_fusion.1), channel_id=1, replica_groups={{0,2,4,6,8,10,12,14},{1,3,5,7,9,11,13,15},{16,18,20,22,24,26,28,30},{17..., dimensions={0} | all-to-all | bytes 393216 | tf_op jit(solution)/shard_map/all_to_all | solution.py:27
  177.9 10.0 %all_to_all.32 = bf16[8,6,768]{2,1,0:T(8,128)(2,1)S(1)} all-to-all(bf16[8,6,768]{2,1,0:T(8,128)(2,1)S(1)} %broadcast_in_dim.38), channel_id=1, replica_groups={{0,2,4,6,8,10,12,14},{1,3,5,7,9,11,13,15},{16,18,20,22,24,26,28,30},{17..., dimensions={0} | all-to-all | bytes 147456 | tf_op jit(solution)/shard_map/all_to_all | solution.py:27
  188.0 18.0 %all_to_all.33 = bf16[16,48,768]{2,1,0:T(8,128)(2,1)} all-to-all(bf16[16,48,768]{2,1,0:T(8,128)(2,1)S(1)} %broadcast_in_dim.40), channel_id=1, replica_groups={{0,16,32,48,64,80,96,112,128,144,160,176,192,208,224,240},{1,17,33,49,6..., dimensions={0} | all-to-all | bytes 2359296 | tf_op jit(solution)/shard_map/all_to_all | solution.py:27
  206.0 5.3 %collective-permute-start.63 = (bf16[768,768]{1,0:T(8,128)(2,1)}, bf16[768,768]{1,0:T(8,128)(2,1)}, u32[]{:S(2)}, u32[]{:S(2)}) collective-permute-start(bf16[768,768]{1,0:T(8,128)(2,1)} %bitcast.15), channel_id=1, source_target_pairs={{0,1},{1,0},{2,3},{3,2},{4,5},{5,4},{6,7},{7,6},{8,9},{9,8},{10,11... | collective-permute-start | bytes 3538952 | tf_op jit(solution)/shard_map/ppermute | solution.py:23
  211.3 1.3 convolution_convert_fusion
  212.6 1.3 convolution_convert_fusion.1
  214.4 4.1 %select_convert_fusion = (f32[768,768]{1,0:T(8,128)}, f32[768,768]{1,0:T(8,128)}) fusion(bf16[768,768]{1,0:T(8,128)(2,1)} %collective-permute-done.63, pred[]{:T(512)S(6)} %eq.22, bf16[16,48,768]{2,1,0:T(8,128)(2,1)} %all_to_all.33), kind=kLoop, calls=%fused_computation.6 | loop fusion | flops 2359296 | bytes 7077889 | tf_op jit(solution)/shard_map/convert_element_type | solution.py:319
  (67 shorter events, 7.2 us)
Async XLA Ops:
  4.8 10.0 %copy-start.16 = (s32[4]{0:T(128)S(1)}, s32[4]{0:T(128)}, u32[]{:S(2)}) copy-start(s32[4]{0:T(128)} %param.49) | copy-start | bytes 52
  4.8 30.9 %collective-permute-start.60 = (bf16[16,32,768]{2,1,0:T(8,128)(2,1)}, bf16[16,32,768]{2,1,0:T(8,128)(2,1)S(1)}, u32[]{:S(2)}, u32[]{:S(2)}) collective-permute-start(bf16[16,32,768]{2,1,0:T(8,128)(2,1)} %get-tuple-element.234.both_ref), channel_id=1, source_target_pairs={{0,255},{1,0},{2,1},{3,2},{4,3},{5,4},{6,5},{7,6},{8,7},{9,8},{10,... | collective-permute-start | bytes 2359304 | tf_op jit(solution)/shard_map/ppermute | solution.py:19
  8.1 27.6 %collective-permute-start.61 = (bf16[16,32,768]{2,1,0:T(8,128)(2,1)}, bf16[16,32,768]{2,1,0:T(8,128)(2,1)S(1)}, u32[]{:S(2)}, u32[]{:S(2)}) collective-permute-start(bf16[16,32,768]{2,1,0:T(8,128)(2,1)} %get-tuple-element.234.both_ref), channel_id=1, source_target_pairs={{0,1},{1,2},{2,3},{3,4},{4,5},{5,6},{6,7},{7,8},{8,9},{9,10},{10,1... | collective-permute-start | bytes 2359304 | tf_op jit(solution)/shard_map/ppermute | solution.py:19
  8.1 27.6 %all-to-all-start = ((bf16[16,32,768]{2,1,0:T(8,128)(2,1)}), bf16[16,32,768]{2,1,0:T(8,128)(2,1)S(1)}, u32[]{:S(2)}, u32[]{:S(2)}) async-start(bf16[16,32,768]{2,1,0:T(8,128)(2,1)} %get-tuple-element.234.both_ref), calls=%async_computation | async-start | bytes 1572864 | tf_op jit(solution)/shard_map/all_to_all | solution.py:27
  35.7 0.9 copy-start.10
  35.7 1.1 copy-start.12
  50.5 12.5 %collective-permute-start.24 = (bf16[16,16,768]{2,1,0:T(8,128)(2,1)S(1)}, bf16[16,16,768]{2,1,0:T(8,128)(2,1)S(1)}, u32[]{:S(2)}, u32[]{:S(2)}) collective-permute-start(bf16[16,16,768]{2,1,0:T(8,128)(2,1)S(1)} %get-tuple-element.177), channel_id=1, source_target_pairs={{0,3},{1,4},{2,5},{3,6},{4,7},{5,8},{6,9},{7,10},{8,11},{9,12},{10... | collective-permute-start | bytes 1179656 | tf_op jit(solution)/shard_map/cond/branch_13_fun/ppermute | solution.py:72
  50.6 15.1 %collective-permute-start.25 = (bf16[16,16,768]{2,1,0:T(8,128)(2,1)S(1)}, bf16[16,16,768]{2,1,0:T(8,128)(2,1)S(1)}, u32[]{:S(2)}, u32[]{:S(2)}) collective-permute-start(bf16[16,16,768]{2,1,0:T(8,128)(2,1)S(1)} %get-tuple-element.178), channel_id=1, source_target_pairs={{0,13},{1,14},{2,15},{3,0},{4,1},{5,2},{6,3},{7,4},{8,5},{9,6},{10... | collective-permute-start | bytes 1179656 | tf_op jit(solution)/shard_map/cond/branch_13_fun/ppermute | solution.py:72
  66.2 27.7 %collective-permute-start.48 = (bf16[16,16,768]{2,1,0:T(8,128)(2,1)S(1)}, bf16[16,16,768]{2,1,0:T(8,128)(2,1)S(1)}, u32[]{:S(2)}, u32[]{:S(2)}) collective-permute-start(bf16[16,16,768]{2,1,0:T(8,128)(2,1)S(1)} %get-tuple-element.201), channel_id=1, source_target_pairs={{0,6},{1,7},{2,8},{3,9},{4,10},{5,11},{6,12},{7,13},{8,14},{9,15},... | collective-permute-start | bytes 1179656 | tf_op jit(solution)/shard_map/cond/branch_10_fun/ppermute | solution.py:72
  68.8 29.0 %collective-permute-start.49 = (bf16[16,16,768]{2,1,0:T(8,128)(2,1)S(1)}, bf16[16,16,768]{2,1,0:T(8,128)(2,1)S(1)}, u32[]{:S(2)}, u32[]{:S(2)}) collective-permute-start(bf16[16,16,768]{2,1,0:T(8,128)(2,1)S(1)} %get-tuple-element.202), channel_id=1, source_target_pairs={{0,10},{1,11},{2,12},{3,13},{4,14},{5,15},{6,0},{7,1},{8,2},{9,3},... | collective-permute-start | bytes 1179656 | tf_op jit(solution)/shard_map/cond/branch_10_fun/ppermute | solution.py:72
  99.7 7.7 %copy-start = (bf16[16,32,768]{2,1,0:T(8,128)(2,1)S(1)}, bf16[16,32,768]{2,1,0:T(8,128)(2,1)}, u32[]{:S(2)}) copy-start(bf16[16,32,768]{2,1,0:T(8,128)(2,1)} %get-tuple-element.234.both_ref) | copy-start | bytes 2359300
  99.7 28.3 %all-to-all-start.1 = ((bf16[16,64,768]{2,1,0:T(8,128)(2,1)}), bf16[16,64,768]{2,1,0:T(8,128)(2,1)S(1)}, u32[]{:S(2)}, u32[]{:S(2)}) async-start(bf16[16,64,768]{2,1,0:T(8,128)(2,1)} %line_up.1), calls=%async_computation.1 | async-start | bytes 3145728 | tf_op jit(solution)/shard_map/all_to_all | solution.py:27
  107.3 1.1 copy-start.11
  108.5 1.1 copy-start.13
  109.6 18.4 %copy-start.4 = (bf16[256,768]{1,0:T(8,128)(2,1)S(1)}, bf16[256,768]{1,0:T(8,128)(2,1)}, u32[]{:S(2)}) copy-start(bf16[256,768]{1,0:T(8,128)(2,1)} %xi_hbm.3) | copy-start | bytes 1179652
  109.6 18.4 %copy-start.5 = (bf16[256,768]{1,0:T(8,128)(2,1)S(1)}, bf16[256,768]{1,0:T(8,128)(2,1)}, u32[]{:S(2)}) copy-start(bf16[256,768]{1,0:T(8,128)(2,1)} %xt_hbm.3) | copy-start | bytes 1179652
  112.2 1.2 copy-start.2
  113.3 0.6 copy-start.8
  128.0 1.4 copy-start.1
  129.4 1.4 copy-start.3
  130.8 0.7 copy-start.9
  135.7 5.7 %copy-start.6 = (bf16[256,768]{1,0:T(8,128)(2,1)}, bf16[256,768]{1,0:T(8,128)(2,1)S(1)}, u32[]{:S(2)}) copy-start(bf16[256,768]{1,0:T(8,128)(2,1)S(1)} %get-tuple-element.247) | copy-start | bytes 1179652
  135.7 5.6 %collective-permute-start.62 = (bf16[784,768]{1,0:T(8,128)(2,1)S(1)}, bf16[784,768]{1,0:T(8,128)(2,1)S(1)}, u32[]{:S(2)}, u32[]{:S(2)}) collective-permute-start(bf16[784,768]{1,0:T(8,128)(2,1)S(1)} %get-tuple-element.249), channel_id=1, source_target_pairs={{0,1},{1,0},{2,3},{3,2},{4,5},{5,4},{6,7},{7,6},{8,9},{9,8},{10,11... | collective-permute-start | bytes 3612680 | tf_op jit(solution)/shard_map/ppermute | solution.py:23
  188.0 23.3 %copy-start.7 = (bf16[256,768]{1,0:T(8,128)(2,1)S(1)}, bf16[256,768]{1,0:T(8,128)(2,1)}, u32[]{:S(2)}) copy-start(bf16[256,768]{1,0:T(8,128)(2,1)} %copy-done.6) | copy-start | bytes 1179652
  188.0 23.3 %copy-start.14 = (bf16[768,768]{1,0:T(8,128)(2,1)S(1)}, bf16[768,768]{1,0:T(8,128)(2,1)}, u32[]{:S(2)}) copy-start(bf16[768,768]{1,0:T(8,128)(2,1)} %wt_hbm.1) | copy-start | bytes 3538948
  206.0 6.6 %copy-start.15 = (bf16[768,768]{1,0:T(8,128)(2,1)S(1)}, bf16[768,768]{1,0:T(8,128)(2,1)}, u32[]{:S(2)}) copy-start(bf16[768,768]{1,0:T(8,128)(2,1)} %wi_hbm.1) | copy-start | bytes 3538948
  206.0 8.4 %collective-permute-start.63 = (bf16[768,768]{1,0:T(8,128)(2,1)}, bf16[768,768]{1,0:T(8,128)(2,1)}, u32[]{:S(2)}, u32[]{:S(2)}) collective-permute-start(bf16[768,768]{1,0:T(8,128)(2,1)} %bitcast.15), channel_id=1, source_target_pairs={{0,1},{1,0},{2,3},{3,2},{4,5},{5,4},{6,7},{7,6},{8,9},{9,8},{10,11... | collective-permute-start | bytes 3538952 | tf_op jit(solution)/shard_map/ppermute | solution.py:23
where the time goes:
time: 221 us; the launch traced here: 219 us
  waiting for transfers between devices  67.1 us (30%)
  blocking collectives  63.3 us (29%)
  starting transfers between devices  32.2 us (15%)
  loops' own time  14.1 us (6%)
  Pallas kernels  12.7 us (6%)
  between operations  10.5 us (5%)
  local copies, waits for them, and re-layouts  10.1 us (5%)
  other arithmetic  6.18 us (3%)
  matrix products  2.5 us (1%)
    all_to_all x4, blocking collectives, exchange(): lax.all_to_all(value, 'pairs', 0, 0, axis_index_groups=groups, tiled=True)  63.3 us
    ppermute x4, waiting for transfers between devices, turned(): return lax.ppermute(value, 'pairs', pairs)  39 us
    all_to_all x2, waiting for transfers between devices, exchange(): lax.all_to_all(value, 'pairs', 0, 0, axis_index_groups=groups, tiled=True)  25.5 us
    another operation x2, loops' own time, along(): return tuple(lax.switch(low, [branch(k) for k in range(STEP)], txt, img))  14.1 us
    all_to_all x2, starting transfers between devices, exchange(): lax.all_to_all(value, 'pairs', 0, 0, axis_index_groups=groups, tiled=True)  12.9 us
    unnamed x34, local copies, waits for them, and re-layouts  8.7 us
    ppermute x2, starting transfers between devices, other_core(): lax.ppermute(value, 'pairs', [(source, source ^ 1) for source in range(CO...  8.37 us
    ppermute x4, starting transfers between devices, turned(): return lax.ppermute(value, 'pairs', pairs)  7.58 us
  transfers between devices with their start and end apart: 10, of which 7 were waited for; matrix products, arithmetic and copies ran while one was open for 2% of the time, Pallas kernels for 1%

commit v1 on v0

--- a/solution.py
+++ b/solution.py
@@ -277,26 +277,29 @@
     )(sb, core, both, far, dz, stats, u, image_feats, text_feats)
 
 
+def terms_of(stats):
+    one = lax.reduce_precision(stats, 8, 7)
+    two = lax.reduce_precision(stats - one, 8, 7)
+    return jnp.concatenate([one, two, stats - one - two]).astype(jnp.bfloat16)
+
+
 def summed_heads(given, kept, total):
     width = kept.shape[1]
     rows = width // (X * Y)
     got = other_core(given).astype(jnp.float32)
     part = (kept[:width] + got[:width]).astype(jnp.bfloat16)
     stats = kept[width, 0:3] + jnp.sum(got[width : width + 3, 0:3], axis=0)
-    one = lax.reduce_precision(stats, 8, 7)
-    two = lax.reduce_precision(stats - one, 8, 7)
-    three = stats - one - two
-    terms = jnp.stack([one, two, three])
-    extra = jnp.zeros((8, width), jnp.bfloat16).at[0:3, 0:3].set(terms.astype(jnp.bfloat16))
+    extra = jnp.zeros((8, width), jnp.bfloat16).at[0, 0:9].set(terms_of(stats))
     plane = jnp.concatenate([part.reshape(X * Y, rows, width), jnp.broadcast_to(extra[None], (X * Y, 8, width))], axis=1)
     plane = exchange(plane, PLANES)
     plane = jnp.sum(plane.astype(jnp.float32), axis=0)
-    stats = jnp.sum(plane[rows : rows + 3, 0:3], axis=0)
+    stats = jnp.sum(plane[rows, 0:9].reshape(3, 3), axis=0)
     few = rows // Z
-    extra = jnp.zeros((8 - few, width), jnp.float32).at[0, 0:3].set(stats)
-    column = jnp.concatenate([plane[:rows].reshape(Z, few, width), jnp.broadcast_to(extra[None], (Z, 8 - few, width))], axis=1)
-    column = jnp.sum(exchange(column, COLUMNS), axis=0) / total
-    stats = column[few, 0:3]
+    extra = jnp.zeros((8 - few, width), jnp.bfloat16).at[0, 0:9].set(terms_of(stats))
+    part = plane[:rows].astype(jnp.bfloat16).reshape(Z, few, width)
+    column = jnp.concatenate([part, jnp.broadcast_to(extra[None], (Z, 8 - few, width))], axis=1)
+    column = jnp.sum(exchange(column, COLUMNS).astype(jnp.float32), axis=0) / total
+    stats = jnp.sum(column[few, 0:9].reshape(3, 3), axis=0)
     part = column[:few].astype(jnp.bfloat16)
     part = exchange(jnp.broadcast_to(part[None], (Z, few, width)), COLUMNS).reshape(rows, width)
     part = exchange(jnp.broadcast_to(part[None], (X * Y, rows, width)), PLANES).reshape(width, width)

time: 221 us -> 221 us (level)
  transfers between devices with their start and end apart: 10 -> 10, of which waited for: 7 -> 6; matrix products, arithmetic and copies ran while one was open for 2% -> 2% of each run, Pallas kernels for 1% -> 1%
where the time goes in v1:
time: 221 us; the launch traced here: 217 us
  waiting for transfers between devices  67.3 us (30%)
  blocking collectives  62.2 us (28%)
  starting transfers between devices  30.5 us (14%)
  loops' own time  14.1 us (6%)
  Pallas kernels  12.7 us (6%)
  between operations  10.4 us (5%)
  local copies, waits for them, and re-layouts  9.85 us (4%)
  other arithmetic  6.88 us (3%)
  matrix products  2.5 us (1%)
    all_to_all x4, blocking collectives, exchange(): lax.all_to_all(value, 'pairs', 0, 0, axis_index_groups=groups, tiled=True)  62.2 us
    ppermute x4, waiting for transfers between devices, turned(): return lax.ppermute(value, 'pairs', pairs)  37.6 us
    all_to_all x2, waiting for transfers between devices, exchange(): lax.all_to_all(value, 'pairs', 0, 0, axis_index_groups=groups, tiled=True)  27.1 us
    another operation x2, loops' own time, along(): return tuple(lax.switch(low, [branch(k) for k in range(STEP)], txt, img))  14.1 us
    all_to_all x2, starting transfers between devices, exchange(): lax.all_to_all(value, 'pairs', 0, 0, axis_index_groups=groups, tiled=True)  10.8 us
    ppermute x4, starting transfers between devices, turned(): return lax.ppermute(value, 'pairs', pairs)  9.24 us
    unnamed x34, local copies, waits for them, and re-layouts  8.7 us
    ppermute x2, starting transfers between devices, other_core(): lax.ppermute(value, 'pairs', [(source, source ^ 1) for source in range(CO...  7.14 us
  transfers between devices with their start and end apart: 10, of which 6 were waited for; matrix products, arithmetic and copies ran while one was open for 2% of the time, Pallas kernels for 1%

profile of v1, /device:TPU:1, one launch (start us, length us, event | category | flops | bytes accessed | tf_op | source)
XLA Modules:
  0.0 216.5 jit_solution(14756163483586315829)
XLA Ops:
  0.6 4.1 %embed.1 = (bf16[16,32,768]{2,1,0:T(8,128)(2,1)}, f32[512,768]{1,0:T(8,128)}) custom-call(bf16[256,768]{1,0:T(8,128)(2,1)} %xi_hbm.3, bf16[256,768]{1,0:T(8,128)(2,1)} %xt_hbm.3, bf16[768,768]{1,0:T(8,128)(2,1)} %wi_hbm.1, bf16[768,768]{1,0:T(8,128)(2,1)} %wt_hbm.1), custom_call_target="tpu_custom_call" | custom-call | tf_op jit(solution)/shard_map/embed/pallas_call | solution.py:52
  4.8 3.3 %collective-permute-start.60 = (bf16[16,32,768]{2,1,0:T(8,128)(2,1)}, bf16[16,32,768]{2,1,0:T(8,128)(2,1)S(1)}, u32[]{:S(2)}, u32[]{:S(2)}) collective-permute-start(bf16[16,32,768]{2,1,0:T(8,128)(2,1)} %get-tuple-element.234.both_ref), channel_id=1, source_target_pairs={{0,255},{1,0},{2,1},{3,2},{4,3},{5,4},{6,5},{7,6},{8,7},{9,8},{10,... | collective-permute-start | bytes 2359304 | tf_op jit(solution)/shard_map/ppermute | solution.py:19
  8.1 6.6 %all-to-all-start = ((bf16[16,32,768]{2,1,0:T(8,128)(2,1)}), bf16[16,32,768]{2,1,0:T(8,128)(2,1)S(1)}, u32[]{:S(2)}, u32[]{:S(2)}) async-start(bf16[16,32,768]{2,1,0:T(8,128)(2,1)} %get-tuple-element.234.both_ref), calls=%async_computation | async-start | bytes 1572864 | tf_op jit(solution)/shard_map/all_to_all | solution.py:27
  24.2 11.5 %all-to-all-done = bf16[16,32,768]{2,1,0:T(8,128)(2,1)S(1)} async-done(((bf16[16,32,768]{2,1,0:T(8,128)(2,1)}), bf16[16,32,768]{2,1,0:T(8,128)(2,1)S(1)}, u32[]{:S(2)}, u32[]{:S(2)}) %all-to-all-start) | async-done | bytes 786464 | tf_op jit(solution)/shard_map/all_to_all | solution.py:27
  36.8 41.0 %conditional.2 = ((bf16[16,16,768]{2,1,0:T(8,128)(2,1)S(1)}, bf16[16,16,768]{2,1,0:T(8,128)(2,1)S(1)})) conditional(s32[]{:T(128)} %clamp.6, (bf16[16,16,768]{2,1,0:T(8,128)(2,1)S(1)}, bf16[16,16,768]{2,1,0:T(8,128)(2,1)S(1)}) %tuple.144, (bf16[16,16,768]{2,1,0:T(8,128)(2,1)S(1)}, ...), branch_computations={%region_1.2_spmd, %region_2.3_spmd, %region_3.4_spmd, %region_4.5_... | conditional | bytes 4718696 | solution.py:81
  50.6 4.5 %collective-permute-start.19 = (bf16[16,16,768]{2,1,0:T(8,128)(2,1)S(1)}, bf16[16,16,768]{2,1,0:T(8,128)(2,1)S(1)}, u32[]{:S(2)}, u32[]{:S(2)}) collective-permute-start(bf16[16,16,768]{2,1,0:T(8,128)(2,1)S(1)} %get-tuple-element.172), channel_id=1, source_target_pairs={{0,10},{1,11},{2,12},{3,13},{4,14},{5,15},{6,0},{7,1},{8,2},{9,3},... | collective-permute-start | bytes 1179656 | tf_op jit(solution)/shard_map/cond/branch_10_fun/ppermute | solution.py:72
  55.0 22.7 %collective-permute-done.18 = bf16[16,16,768]{2,1,0:T(8,128)(2,1)S(1)} collective-permute-done((bf16[16,16,768]{2,1,0:T(8,128)(2,1)S(1)}, bf16[16,16,768]{2,1,0:T(8,128)(2,1)S(1)}, u32[]{:S(2)}, u32[]{:S(2)}) %collective-permute-start.18) | collective-permute-done | bytes 393248 | tf_op jit(solution)/shard_map/cond/branch_10_fun/ppermute | solution.py:72
  77.9 20.1 %conditional.3 = ((bf16[16,16,768]{2,1,0:T(8,128)(2,1)S(1)}, bf16[16,16,768]{2,1,0:T(8,128)(2,1)S(1)})) conditional(s32[]{:T(128)} %clamp.7, (bf16[16,16,768]{2,1,0:T(8,128)(2,1)S(1)}, bf16[16,16,768]{2,1,0:T(8,128)(2,1)S(1)}) %tuple.145, (bf16[16,16,768]{2,1,0:T(8,128)(2,1)S(1)}, ...), branch_computations={%region_17.18_spmd, %region_18.19_spmd, %region_19.20_spmd, %regio... | conditional | bytes 4718696 | solution.py:81
  78.4 3.8 %collective-permute-start.54 = (bf16[16,16,768]{2,1,0:T(8,128)(2,1)S(1)}, bf16[16,16,768]{2,1,0:T(8,128)(2,1)S(1)}, u32[]{:S(2)}, u32[]{:S(2)}) collective-permute-start(bf16[16,16,768]{2,1,0:T(8,128)(2,1)S(1)} %get-tuple-element.207), channel_id=1, source_target_pairs={{0,3},{1,4},{2,5},{3,6},{4,7},{5,8},{6,9},{7,10},{8,11},{9,12},{10... | collective-permute-start | bytes 1179656 | tf_op jit(solution)/shard_map/cond/branch_13_fun/ppermute | solution.py:72
  82.2 0.9 collective-permute-start.55
  83.1 12.3 %collective-permute-done.54 = bf16[16,16,768]{2,1,0:T(8,128)(2,1)S(1)} collective-permute-done((bf16[16,16,768]{2,1,0:T(8,128)(2,1)S(1)}, bf16[16,16,768]{2,1,0:T(8,128)(2,1)S(1)}, u32[]{:S(2)}, u32[]{:S(2)}) %collective-permute-start.54) | collective-permute-done | bytes 393248 | tf_op jit(solution)/shard_map/cond/branch_13_fun/ppermute | solution.py:72
  95.4 2.6 %collective-permute-done.55 = bf16[16,16,768]{2,1,0:T(8,128)(2,1)S(1)} collective-permute-done((bf16[16,16,768]{2,1,0:T(8,128)(2,1)S(1)}, bf16[16,16,768]{2,1,0:T(8,128)(2,1)S(1)}, u32[]{:S(2)}, u32[]{:S(2)}) %collective-permute-start.55) | collective-permute-done | bytes 393248 | tf_op jit(solution)/shard_map/cond/branch_13_fun/ppermute | solution.py:72
  98.1 1.8 line_up.1
  99.9 4.2 %all-to-all-start.1 = ((bf16[16,64,768]{2,1,0:T(8,128)(2,1)}), bf16[16,64,768]{2,1,0:T(8,128)(2,1)S(1)}, u32[]{:S(2)}, u32[]{:S(2)}) async-start(bf16[16,64,768]{2,1,0:T(8,128)(2,1)} %line_up.1), calls=%async_computation.1 | async-start | bytes 3145728 | tf_op jit(solution)/shard_map/all_to_all | solution.py:27
  105.5 1.1 copy-done.11
  106.7 1.1 copy-done.13
  107.8 2.5 %near.1 = (f32[2,256,768]{2,1,0:T(8,128)S(1)}, f32[3,8,256]{2,1,0:T(8,128)S(1)}) custom-call(f32[2]{0:T(128)S(1)} %pad_maximum_fusion.2.sb_ref, bf16[16,32,768]{2,1,0:T(8,128)(2,1)S(1)} %copy-done, bf16[16,32,768]{2,1,0:T(8,128)(2,1)S(1)} %copy-done.11, bf16[16,32,768]{2,1,0:T(8,128)(2,1)S(1)} %copy-done.13), custom_call_target="tpu_custom_call" | custom-call | flops 1509949440 | bytes 3145728 | tf_op jit(solution)/shard_map/near/pallas_call | solution.py:190
  110.3 1.2 copy-done.2
  112.1 15.6 %all-to-all-done.1.far_ref = bf16[16,64,768]{2,1,0:T(8,128)(2,1)S(1)} async-done(((bf16[16,64,768]{2,1,0:T(8,128)(2,1)}), bf16[16,64,768]{2,1,0:T(8,128)(2,1)S(1)}, u32[]{:S(2)}, u32[]{:S(2)}) %all-to-all-start.1) | async-done | bytes 1572896 | tf_op jit(solution)/shard_map/all_to_all | solution.py:27
  127.7 1.4 copy-done.1
  129.2 1.4 copy-done.3
  131.3 4.2 %last.1 = (bf16[256,768]{1,0:T(8,128)(2,1)S(1)}, bf16[256,768]{1,0:T(8,128)(2,1)S(1)}, f32[776,768]{1,0:T(8,128)S(1)}, bf16[784,768]{1,0:T(8,128)(2,1)S(1)}) custom-call(f32[2]{0:T(128)S(1)} %pad_maximum_fusion.2.sb_ref, s32[1]{0:T(128)} %bitcast.core_ref, bf16[16,32,768]{2,1,0:T(8,128)(2,1)S(1)} %copy-done, ...), custom_call_target="tpu_custom_call" | custom-call | tf_op jit(solution)/shard_map/last/pallas_call | solution.py:260
  135.5 1.8 collective-permute-start.62
  137.3 2.5 %collective-permute-done.62 = bf16[784,768]{1,0:T(8,128)(2,1)S(1)} collective-permute-done((bf16[784,768]{1,0:T(8,128)(2,1)S(1)}, bf16[784,768]{1,0:T(8,128)(2,1)S(1)}, u32[]{:S(2)}, u32[]{:S(2)}) %collective-permute-start.62) | collective-permute-done | bytes 1204256 | tf_op jit(solution)/shard_map/ppermute | solution.py:23
  140.8 22.6 %all_to_all.30 = bf16[16,56,768]{2,1,0:T(8,128)(2,1)S(1)} all-to-all(bf16[16,56,768]{2,1,0:T(8,128)(2,1)S(1)} %pad_maximum_fusion), channel_id=1, replica_groups={{0,16,32,48,64,80,96,112,128,144,160,176,192,208,224,240},{1,17,33,49,6..., dimensions={0} | all-to-all | bytes 2752512 | tf_op jit(solution)/shard_map/all_to_all | solution.py:27
  163.9 11.6 %all_to_all.31 = bf16[8,8,768]{2,1,0:T(8,128)(2,1)S(1)} all-to-all(bf16[8,8,768]{2,1,0:T(8,128)(2,1)S(1)} %pad_maximum_fusion.1), channel_id=1, replica_groups={{0,2,4,6,8,10,12,14},{1,3,5,7,9,11,13,15},{16,18,20,22,24,26,28,30},{17..., dimensions={0} | all-to-all | bytes 196608 | tf_op jit(solution)/shard_map/all_to_all | solution.py:27
  175.6 10.0 %all_to_all.32 = bf16[8,6,768]{2,1,0:T(8,128)(2,1)S(1)} all-to-all(bf16[8,6,768]{2,1,0:T(8,128)(2,1)S(1)} %broadcast_in_dim.35), channel_id=1, replica_groups={{0,2,4,6,8,10,12,14},{1,3,5,7,9,11,13,15},{16,18,20,22,24,26,28,30},{17..., dimensions={0} | all-to-all | bytes 147456 | tf_op jit(solution)/shard_map/all_to_all | solution.py:27
  185.7 18.1 %all_to_all.33 = bf16[16,48,768]{2,1,0:T(8,128)(2,1)} all-to-all(bf16[16,48,768]{2,1,0:T(8,128)(2,1)S(1)} %broadcast_in_dim.37), channel_id=1, replica_groups={{0,16,32,48,64,80,96,112,128,144,160,176,192,208,224,240},{1,17,33,49,6..., dimensions={0} | all-to-all | bytes 2359296 | tf_op jit(solution)/shard_map/all_to_all | solution.py:27
  203.8 5.3 %collective-permute-start.63 = (bf16[768,768]{1,0:T(8,128)(2,1)}, bf16[768,768]{1,0:T(8,128)(2,1)}, u32[]{:S(2)}, u32[]{:S(2)}) collective-permute-start(bf16[768,768]{1,0:T(8,128)(2,1)} %bitcast.17), channel_id=1, source_target_pairs={{0,1},{1,0},{2,3},{3,2},{4,5},{5,4},{6,7},{7,6},{8,9},{9,8},{10,11... | collective-permute-start | bytes 3538952 | tf_op jit(solution)/shard_map/ppermute | solution.py:23
  209.1 1.3 convolution_convert_fusion
  210.3 1.3 convolution_convert_fusion.1
  212.2 4.1 %select_convert_fusion = (f32[768,768]{1,0:T(8,128)}, f32[768,768]{1,0:T(8,128)}) fusion(bf16[768,768]{1,0:T(8,128)(2,1)} %collective-permute-done.63, pred[]{:T(512)S(6)} %eq.22, bf16[16,48,768]{2,1,0:T(8,128)(2,1)} %all_to_all.33), kind=kLoop, calls=%fused_computation.6 | loop fusion | flops 2359296 | bytes 7077889 | tf_op jit(solution)/shard_map/convert_element_type | solution.py:322
  (72 shorter events, 6.5 us)
Async XLA Ops:
  4.8 10.0 %copy-start.16 = (s32[4]{0:T(128)S(1)}, s32[4]{0:T(128)}, u32[]{:S(2)}) copy-start(s32[4]{0:T(128)} %param.49) | copy-start | bytes 52
  4.8 30.9 %collective-permute-start.60 = (bf16[16,32,768]{2,1,0:T(8,128)(2,1)}, bf16[16,32,768]{2,1,0:T(8,128)(2,1)S(1)}, u32[]{:S(2)}, u32[]{:S(2)}) collective-permute-start(bf16[16,32,768]{2,1,0:T(8,128)(2,1)} %get-tuple-element.234.both_ref), channel_id=1, source_target_pairs={{0,255},{1,0},{2,1},{3,2},{4,3},{5,4},{6,5},{7,6},{8,7},{9,8},{10,... | collective-permute-start | bytes 2359304 | tf_op jit(solution)/shard_map/ppermute | solution.py:19
  8.1 27.6 %collective-permute-start.61 = (bf16[16,32,768]{2,1,0:T(8,128)(2,1)}, bf16[16,32,768]{2,1,0:T(8,128)(2,1)S(1)}, u32[]{:S(2)}, u32[]{:S(2)}) collective-permute-start(bf16[16,32,768]{2,1,0:T(8,128)(2,1)} %get-tuple-element.234.both_ref), channel_id=1, source_target_pairs={{0,1},{1,2},{2,3},{3,4},{4,5},{5,6},{6,7},{7,8},{8,9},{9,10},{10,1... | collective-permute-start | bytes 2359304 | tf_op jit(solution)/shard_map/ppermute | solution.py:19
  8.1 27.6 %all-to-all-start = ((bf16[16,32,768]{2,1,0:T(8,128)(2,1)}), bf16[16,32,768]{2,1,0:T(8,128)(2,1)S(1)}, u32[]{:S(2)}, u32[]{:S(2)}) async-start(bf16[16,32,768]{2,1,0:T(8,128)(2,1)} %get-tuple-element.234.both_ref), calls=%async_computation | async-start | bytes 1572864 | tf_op jit(solution)/shard_map/all_to_all | solution.py:27
  35.7 0.9 copy-start.10
  35.7 1.1 copy-start.12
  50.5 27.3 %collective-permute-start.18 = (bf16[16,16,768]{2,1,0:T(8,128)(2,1)S(1)}, bf16[16,16,768]{2,1,0:T(8,128)(2,1)S(1)}, u32[]{:S(2)}, u32[]{:S(2)}) collective-permute-start(bf16[16,16,768]{2,1,0:T(8,128)(2,1)S(1)} %get-tuple-element.171), channel_id=1, source_target_pairs={{0,6},{1,7},{2,8},{3,9},{4,10},{5,11},{6,12},{7,13},{8,14},{9,15},... | collective-permute-start | bytes 1179656 | tf_op jit(solution)/shard_map/cond/branch_10_fun/ppermute | solution.py:72
  50.6 27.2 %collective-permute-start.19 = (bf16[16,16,768]{2,1,0:T(8,128)(2,1)S(1)}, bf16[16,16,768]{2,1,0:T(8,128)(2,1)S(1)}, u32[]{:S(2)}, u32[]{:S(2)}) collective-permute-start(bf16[16,16,768]{2,1,0:T(8,128)(2,1)S(1)} %get-tuple-element.172), channel_id=1, source_target_pairs={{0,10},{1,11},{2,12},{3,13},{4,14},{5,15},{6,0},{7,1},{8,2},{9,3},... | collective-permute-start | bytes 1179656 | tf_op jit(solution)/shard_map/cond/branch_10_fun/ppermute | solution.py:72
  78.4 17.0 %collective-permute-start.54 = (bf16[16,16,768]{2,1,0:T(8,128)(2,1)S(1)}, bf16[16,16,768]{2,1,0:T(8,128)(2,1)S(1)}, u32[]{:S(2)}, u32[]{:S(2)}) collective-permute-start(bf16[16,16,768]{2,1,0:T(8,128)(2,1)S(1)} %get-tuple-element.207), channel_id=1, source_target_pairs={{0,3},{1,4},{2,5},{3,6},{4,7},{5,8},{6,9},{7,10},{8,11},{9,12},{10... | collective-permute-start | bytes 1179656 | tf_op jit(solution)/shard_map/cond/branch_13_fun/ppermute | solution.py:72
  82.2 15.8 %collective-permute-start.55 = (bf16[16,16,768]{2,1,0:T(8,128)(2,1)S(1)}, bf16[16,16,768]{2,1,0:T(8,128)(2,1)S(1)}, u32[]{:S(2)}, u32[]{:S(2)}) collective-permute-start(bf16[16,16,768]{2,1,0:T(8,128)(2,1)S(1)} %get-tuple-element.208), channel_id=1, source_target_pairs={{0,13},{1,14},{2,15},{3,0},{4,1},{5,2},{6,3},{7,4},{8,5},{9,6},{10... | collective-permute-start | bytes 1179656 | tf_op jit(solution)/shard_map/cond/branch_13_fun/ppermute | solution.py:72
  99.9 5.6 %copy-start = (bf16[16,32,768]{2,1,0:T(8,128)(2,1)S(1)}, bf16[16,32,768]{2,1,0:T(8,128)(2,1)}, u32[]{:S(2)}) copy-start(bf16[16,32,768]{2,1,0:T(8,128)(2,1)} %get-tuple-element.234.both_ref) | copy-start | bytes 2359300
  99.9 27.8 %all-to-all-start.1 = ((bf16[16,64,768]{2,1,0:T(8,128)(2,1)}), bf16[16,64,768]{2,1,0:T(8,128)(2,1)S(1)}, u32[]{:S(2)}, u32[]{:S(2)}) async-start(bf16[16,64,768]{2,1,0:T(8,128)(2,1)} %line_up.1), calls=%async_computation.1 | async-start | bytes 3145728 | tf_op jit(solution)/shard_map/all_to_all | solution.py:27
  105.5 1.1 copy-start.11
  106.7 1.1 copy-start.13
  107.8 20.0 %copy-start.4 = (bf16[256,768]{1,0:T(8,128)(2,1)S(1)}, bf16[256,768]{1,0:T(8,128)(2,1)}, u32[]{:S(2)}) copy-start(bf16[256,768]{1,0:T(8,128)(2,1)} %xi_hbm.3) | copy-start | bytes 1179652
  107.8 20.0 %copy-start.5 = (bf16[256,768]{1,0:T(8,128)(2,1)S(1)}, bf16[256,768]{1,0:T(8,128)(2,1)}, u32[]{:S(2)}) copy-start(bf16[256,768]{1,0:T(8,128)(2,1)} %xt_hbm.3) | copy-start | bytes 1179652
  110.3 1.2 copy-start.2
  111.5 0.6 copy-start.8
  127.7 1.4 copy-start.1
  129.2 1.4 copy-start.3
  130.6 0.7 copy-start.9
  135.5 4.5 %copy-start.6 = (bf16[256,768]{1,0:T(8,128)(2,1)}, bf16[256,768]{1,0:T(8,128)(2,1)S(1)}, u32[]{:S(2)}) copy-start(bf16[256,768]{1,0:T(8,128)(2,1)S(1)} %get-tuple-element.247) | copy-start | bytes 1179652
  135.5 4.3 %collective-permute-start.62 = (bf16[784,768]{1,0:T(8,128)(2,1)S(1)}, bf16[784,768]{1,0:T(8,128)(2,1)S(1)}, u32[]{:S(2)}, u32[]{:S(2)}) collective-permute-start(bf16[784,768]{1,0:T(8,128)(2,1)S(1)} %get-tuple-element.249), channel_id=1, source_target_pairs={{0,1},{1,0},{2,3},{3,2},{4,5},{5,4},{6,7},{7,6},{8,9},{9,8},{10,11... | collective-permute-start | bytes 3612680 | tf_op jit(solution)/shard_map/ppermute | solution.py:23
  185.6 23.5 %copy-start.7 = (bf16[256,768]{1,0:T(8,128)(2,1)S(1)}, bf16[256,768]{1,0:T(8,128)(2,1)}, u32[]{:S(2)}) copy-start(bf16[256,768]{1,0:T(8,128)(2,1)} %copy-done.6) | copy-start | bytes 1179652
  185.6 23.4 %copy-start.14 = (bf16[768,768]{1,0:T(8,128)(2,1)S(1)}, bf16[768,768]{1,0:T(8,128)(2,1)}, u32[]{:S(2)}) copy-start(bf16[768,768]{1,0:T(8,128)(2,1)} %wt_hbm.1) | copy-start | bytes 3538948
  203.8 6.6 %copy-start.15 = (bf16[768,768]{1,0:T(8,128)(2,1)S(1)}, bf16[768,768]{1,0:T(8,128)(2,1)}, u32[]{:S(2)}) copy-start(bf16[768,768]{1,0:T(8,128)(2,1)} %wi_hbm.1) | copy-start | bytes 3538948
  203.8 8.5 %collective-permute-start.63 = (bf16[768,768]{1,0:T(8,128)(2,1)}, bf16[768,768]{1,0:T(8,128)(2,1)}, u32[]{:S(2)}, u32[]{:S(2)}) collective-permute-start(bf16[768,768]{1,0:T(8,128)(2,1)} %bitcast.17), channel_id=1, source_target_pairs={{0,1},{1,0},{2,3},{3,2},{4,5},{5,4},{6,7},{7,6},{8,9},{9,8},{10,11... | collective-permute-start | bytes 3538952 | tf_op jit(solution)/shard_map/ppermute | solution.py:23

commit v2 on v1

--- a/solution.py
+++ b/solution.py
@@ -1,3 +1,5 @@
+import functools
+
 import jax
 import jax.numpy as jnp
 from jax import lax
@@ -283,12 +285,11 @@
     return jnp.concatenate([one, two, stats - one - two]).astype(jnp.bfloat16)
 
 
-def summed_heads(given, kept, total):
+def summed_heads(got, kept, total):
     width = kept.shape[1]
     rows = width // (X * Y)
-    got = other_core(given).astype(jnp.float32)
-    part = (kept[:width] + got[:width]).astype(jnp.bfloat16)
-    stats = kept[width, 0:3] + jnp.sum(got[width : width + 3, 0:3], axis=0)
+    part = (kept[:width] + got[:width].astype(jnp.float32)).astype(jnp.bfloat16)
+    stats = kept[width, 0:3] + jnp.sum(got[width : width + 3, 0:3].astype(jnp.float32), axis=0)
     extra = jnp.zeros((8, width), jnp.bfloat16).at[0, 0:9].set(terms_of(stats))
     plane = jnp.concatenate([part.reshape(X * Y, rows, width), jnp.broadcast_to(extra[None], (X * Y, 8, width))], axis=1)
     plane = exchange(plane, PLANES)
@@ -306,6 +307,45 @@
     return part, stats
 
 
+def write_kernel(turn, core_ref, part_ref, *refs):
+    img_hbm, txt_hbm, wide_ref, sems = refs[-4:]
+    rows = part_ref.shape[0] // sems.shape[0]
+
+    def write(out_hbm):
+        copies = []
+        for k in range(sems.shape[0]):
+            at = slice(k * rows, (k + 1) * rows)
+            wide_ref[at, :] = part_ref[at, :].astype(jnp.float32)
+            copies.append(pltpu.make_async_copy(wide_ref.at[at, :], out_hbm.at[at, :], sems.at[k]))
+            copies[-1].start()
+        for copy in copies:
+            copy.wait()
+
+    @pl.when(core_ref[0] == turn)
+    def _():
+        write(img_hbm)
+
+    @pl.when(core_ref[0] != turn)
+    def _():
+        write(txt_hbm)
+
+
+def write_head(turn, core, part, outs=()):
+    width = part.shape[1]
+    hbm = pl.BlockSpec(memory_space=pl.ANY)
+    return pl.pallas_call(
+        functools.partial(write_kernel, turn),
+        out_shape=(jax.ShapeDtypeStruct(part.shape, jnp.float32),) * 2,
+        in_specs=[pl.BlockSpec(memory_space=pltpu.SMEM), pl.BlockSpec(memory_space=pltpu.VMEM)] + [hbm] * len(outs),
+        out_specs=(hbm, hbm),
+        scratch_shapes=[pltpu.VMEM(part.shape, jnp.float32), pltpu.SemaphoreType.DMA((8,))],
+        input_output_aliases={2 + k: k for k in range(len(outs))},
+        compiler_params=pltpu.CompilerParams(vmem_limit_bytes=16 * 1024 * 1024),
+        cost_estimate=pl.CostEstimate(flops=width * width, bytes_accessed=6 * width * width, transcendentals=0),
+        name="write_head",
+    )(core, part, *outs)
+
+
 def local(image_feats, text_feats, image_head, text_head, logit_scale, logit_bias, round_offsets):
     total = float(COUNT * image_feats.shape[0])
     both, u = embed(image_feats, text_feats, image_head, text_head)
@@ -315,14 +355,12 @@
     core = lax.axis_index("pairs") % CORES
     dz, stats = near(sb, both, ahead, behind)
     du_img, du_txt, kept, given = last(sb, core.reshape(1), both, far, dz, stats, u, image_feats, text_feats)
-    part, sum_stats = summed_heads(given, kept, total)
-    first = core == 0
-    theirs = other_core(part)
-    sum_wi = jnp.where(first, part, theirs).astype(jnp.float32)
-    sum_wt = jnp.where(first, theirs, part).astype(jnp.float32)
-
     g_img = jnp.dot(du_img, image_head.T, preferred_element_type=jnp.float32).astype(jnp.bfloat16)
     g_txt = jnp.dot(du_txt, text_head.T, preferred_element_type=jnp.float32).astype(jnp.bfloat16)
+    got, g_img, g_txt = lax.optimization_barrier((other_core(given), g_img, g_txt))
+    part, sum_stats = summed_heads(got, kept, total)
+    theirs, outs = lax.optimization_barrier((other_core(part), write_head(0, core.reshape(1), part)))
+    sum_wi, sum_wt = write_head(1, core.reshape(1), theirs, outs)
     return (g_img, g_txt, sum_wi, sum_wt, sum_stats)
 
 

time: 221 us -> 210 us (0.950)
  waiting for transfers between devices: 67.3 us -> 61.1 us
  other arithmetic: 6.88 us -> 2.42 us
  Pallas kernels: 12.7 us -> 15.7 us
  starting transfers between devices: 30.5 us -> 27.5 us
    convert_element_type x3 -> x1, other arithmetic: 4.79 us -> 0.33 us  [summed_heads(): part = (kept[:width] + got[:width].astype(jnp.float32)).astype(jnp.bfloat16)]
    all_to_all x2, waiting for transfers between devices: 27.1 us -> 24 us  [exchange(): lax.all_to_all(value, 'pairs', 0, 0, axis_index_groups=groups, tiled=True)]
    pallas_call x0 -> x2, Pallas kernels: none -> 2.96 us  [write_head(): pl.pallas_call(functools.partial(write_kernel, turn), out_shape=(jax.Shap...]
    ppermute x4, starting transfers between devices: 9.24 us -> 6.9 us  [turned(): return lax.ppermute(value, 'pairs', pairs)]
    unnamed x34 -> x26, local copies, waits for them, and re-layouts: 8.7 us -> 7.36 us
  transfers between devices with their start and end apart: 10 -> 10, of which waited for: 6 -> 8; matrix products, arithmetic and copies ran while one was open for 2% -> 2% of each run, Pallas kernels for 1% -> 2%
where the time goes in v2:
time: 210 us; the launch traced here: 206 us
  blocking collectives  63.5 us (30%)
  waiting for transfers between devices  61.1 us (29%)
  starting transfers between devices  27.5 us (13%)
  Pallas kernels  15.7 us (7%)
  loops' own time  14.4 us (7%)
  between operations  10.5 us (5%)
  local copies, waits for them, and re-layouts  8.51 us (4%)
  matrix products  2.51 us (1%)
  other arithmetic  2.42 us (1%)
    all_to_all x4, blocking collectives, exchange(): lax.all_to_all(value, 'pairs', 0, 0, axis_index_groups=groups, tiled=True)  63.5 us
    ppermute x4, waiting for transfers between devices, turned(): return lax.ppermute(value, 'pairs', pairs)  36.5 us
    all_to_all x2, waiting for transfers between devices, exchange(): lax.all_to_all(value, 'pairs', 0, 0, axis_index_groups=groups, tiled=True)  24 us
    another operation x2, loops' own time, along(): return tuple(lax.switch(low, [branch(k) for k in range(STEP)], txt, img))  14.4 us
    all_to_all x2, starting transfers between devices, exchange(): lax.all_to_all(value, 'pairs', 0, 0, axis_index_groups=groups, tiled=True)  11.7 us
    unnamed x26, local copies, waits for them, and re-layouts  7.36 us
    ppermute x4, starting transfers between devices, turned(): return lax.ppermute(value, 'pairs', pairs)  6.9 us
    ppermute x2, starting transfers between devices, other_core(): lax.ppermute(value, 'pairs', [(source, source ^ 1) for source in range(CO...  5.42 us
  transfers between devices with their start and end apart: 10, of which 8 were waited for; matrix products, arithmetic and copies ran while one was open for 2% of the time, Pallas kernels for 2%

profile of v2, /device:TPU:1, one launch (start us, length us, event | category | flops | bytes accessed | tf_op | source)
XLA Modules:
  0.0 206.0 jit_solution(14955844259928994684)
XLA Ops:
  0.6 4.1 %embed.1 = (bf16[16,32,768]{2,1,0:T(8,128)(2,1)}, f32[512,768]{1,0:T(8,128)}) custom-call(bf16[256,768]{1,0:T(8,128)(2,1)} %xi_hbm.3, bf16[256,768]{1,0:T(8,128)(2,1)} %xt_hbm.3, bf16[768,768]{1,0:T(8,128)(2,1)} %wi_hbm.1, bf16[768,768]{1,0:T(8,128)(2,1)} %wt_hbm.1), custom_call_target="tpu_custom_call" | custom-call | tf_op jit(solution)/shard_map/embed/pallas_call | solution.py:54
  4.8 3.1 %collective-permute-start.61 = (bf16[16,32,768]{2,1,0:T(8,128)(2,1)}, bf16[16,32,768]{2,1,0:T(8,128)(2,1)S(1)}, u32[]{:S(2)}, u32[]{:S(2)}) collective-permute-start(bf16[16,32,768]{2,1,0:T(8,128)(2,1)} %get-tuple-element.244.both_ref), channel_id=1, source_target_pairs={{0,1},{1,2},{2,3},{3,4},{4,5},{5,6},{6,7},{7,8},{8,9},{9,10},{10,1... | collective-permute-start | bytes 2359304 | tf_op jit(solution)/shard_map/ppermute | solution.py:21
  8.2 6.4 %all-to-all-start = ((bf16[16,32,768]{2,1,0:T(8,128)(2,1)}), bf16[16,32,768]{2,1,0:T(8,128)(2,1)S(1)}, u32[]{:S(2)}, u32[]{:S(2)}) async-start(bf16[16,32,768]{2,1,0:T(8,128)(2,1)} %get-tuple-element.244.both_ref), calls=%async_computation | async-start | bytes 1572864 | tf_op jit(solution)/shard_map/all_to_all | solution.py:29
  24.1 9.5 %all-to-all-done = bf16[16,32,768]{2,1,0:T(8,128)(2,1)S(1)} async-done(((bf16[16,32,768]{2,1,0:T(8,128)(2,1)}), bf16[16,32,768]{2,1,0:T(8,128)(2,1)S(1)}, u32[]{:S(2)}, u32[]{:S(2)}) %all-to-all-start) | async-done | bytes 786464 | tf_op jit(solution)/shard_map/all_to_all | solution.py:29
  34.7 39.8 %conditional.2 = ((bf16[16,16,768]{2,1,0:T(8,128)(2,1)S(1)}, bf16[16,16,768]{2,1,0:T(8,128)(2,1)S(1)})) conditional(s32[]{:T(128)} %clamp.6, (bf16[16,16,768]{2,1,0:T(8,128)(2,1)S(1)}, bf16[16,16,768]{2,1,0:T(8,128)(2,1)S(1)}) %tuple.146, (bf16[16,16,768]{2,1,0:T(8,128)(2,1)S(1)}, ...), branch_computations={%region_1.2_spmd, %region_2.3_spmd, %region_3.4_spmd, %region_4.5_... | conditional | bytes 4718696 | solution.py:83
  34.7 1.3 collective-permute-start.8
  36.1 2.2 %collective-permute-start.9 = (bf16[16,16,768]{2,1,0:T(8,128)(2,1)S(1)}, bf16[16,16,768]{2,1,0:T(8,128)(2,1)S(1)}, u32[]{:S(2)}, u32[]{:S(2)}) collective-permute-start(bf16[16,16,768]{2,1,0:T(8,128)(2,1)S(1)} %get-tuple-element.162), channel_id=1, source_target_pairs={{0,5},{1,6},{2,7},{3,8},{4,9},{5,10},{6,11},{7,12},{8,13},{9,14},{... | collective-permute-start | bytes 1179656 | tf_op jit(solution)/shard_map/cond/branch_5_fun/ppermute | solution.py:74
  38.3 19.6 %collective-permute-done.8 = bf16[16,16,768]{2,1,0:T(8,128)(2,1)S(1)} collective-permute-done((bf16[16,16,768]{2,1,0:T(8,128)(2,1)S(1)}, bf16[16,16,768]{2,1,0:T(8,128)(2,1)S(1)}, u32[]{:S(2)}, u32[]{:S(2)}) %collective-permute-start.8) | collective-permute-done | bytes 393248 | tf_op jit(solution)/shard_map/cond/branch_5_fun/ppermute | solution.py:74
  58.0 2.6 %collective-permute-done.9 = bf16[16,16,768]{2,1,0:T(8,128)(2,1)S(1)} collective-permute-done((bf16[16,16,768]{2,1,0:T(8,128)(2,1)S(1)}, bf16[16,16,768]{2,1,0:T(8,128)(2,1)S(1)}, u32[]{:S(2)}, u32[]{:S(2)}) %collective-permute-start.9) | collective-permute-done | bytes 393248 | tf_op jit(solution)/shard_map/cond/branch_5_fun/ppermute | solution.py:74
  74.6 18.1 %conditional.3 = ((bf16[16,16,768]{2,1,0:T(8,128)(2,1)S(1)}, bf16[16,16,768]{2,1,0:T(8,128)(2,1)S(1)})) conditional(s32[]{:T(128)} %clamp.7, (bf16[16,16,768]{2,1,0:T(8,128)(2,1)S(1)}, bf16[16,16,768]{2,1,0:T(8,128)(2,1)S(1)}) %tuple.147, (bf16[16,16,768]{2,1,0:T(8,128)(2,1)S(1)}, ...), branch_computations={%region_17.18_spmd, %region_18.19_spmd, %region_19.20_spmd, %regio... | conditional | bytes 4718696 | solution.py:83
  75.2 2.8 %collective-permute-start.35 = (bf16[16,16,768]{2,1,0:T(8,128)(2,1)S(1)}, bf16[16,16,768]{2,1,0:T(8,128)(2,1)S(1)}, u32[]{:S(2)}, u32[]{:S(2)}) collective-permute-start(bf16[16,16,768]{2,1,0:T(8,128)(2,1)S(1)} %get-tuple-element.188), channel_id=1, source_target_pairs={{0,3},{1,4},{2,5},{3,6},{4,7},{5,8},{6,9},{7,10},{8,11},{9,12},{10... | collective-permute-start | bytes 1179656 | tf_op jit(solution)/shard_map/cond/branch_3_fun/ppermute | solution.py:74
  78.0 10.3 %collective-permute-done.34 = bf16[16,16,768]{2,1,0:T(8,128)(2,1)S(1)} collective-permute-done((bf16[16,16,768]{2,1,0:T(8,128)(2,1)S(1)}, bf16[16,16,768]{2,1,0:T(8,128)(2,1)S(1)}, u32[]{:S(2)}, u32[]{:S(2)}) %collective-permute-start.34) | collective-permute-done | bytes 393248 | tf_op jit(solution)/shard_map/cond/branch_3_fun/ppermute | solution.py:74
  88.3 3.9 %collective-permute-done.35 = bf16[16,16,768]{2,1,0:T(8,128)(2,1)S(1)} collective-permute-done((bf16[16,16,768]{2,1,0:T(8,128)(2,1)S(1)}, bf16[16,16,768]{2,1,0:T(8,128)(2,1)S(1)}, u32[]{:S(2)}, u32[]{:S(2)}) %collective-permute-start.35) | collective-permute-done | bytes 393248 | tf_op jit(solution)/shard_map/cond/branch_3_fun/ppermute | solution.py:74
  92.7 1.8 line_up.1
  94.5 5.3 %all-to-all-start.1 = ((bf16[16,64,768]{2,1,0:T(8,128)(2,1)}), bf16[16,64,768]{2,1,0:T(8,128)(2,1)S(1)}, u32[]{:S(2)}, u32[]{:S(2)}) async-start(bf16[16,64,768]{2,1,0:T(8,128)(2,1)} %line_up.1), calls=%async_computation.1 | async-start | bytes 3145728 | tf_op jit(solution)/shard_map/all_to_all | solution.py:29
  101.2 1.1 copy-done.7
  102.4 1.1 copy-done.9
  103.5 2.5 %near.1 = (f32[2,256,768]{2,1,0:T(8,128)S(1)}, f32[3,8,256]{2,1,0:T(8,128)S(1)}) custom-call(f32[2]{0:T(128)S(1)} %pad_maximum_fusion.2.sb_ref, bf16[16,32,768]{2,1,0:T(8,128)(2,1)S(1)} %copy-done, bf16[16,32,768]{2,1,0:T(8,128)(2,1)S(1)} %copy-done.9, bf16[16,32,768]{2,1,0:T(8,128)(2,1)S(1)} %copy-done.7), custom_call_target="tpu_custom_call" | custom-call | flops 1509949440 | bytes 3145728 | tf_op jit(solution)/shard_map/near/pallas_call | solution.py:192
  106.1 1.2 copy-done.2
  107.2 14.5 %all-to-all-done.1.far_ref = bf16[16,64,768]{2,1,0:T(8,128)(2,1)S(1)} async-done(((bf16[16,64,768]{2,1,0:T(8,128)(2,1)}), bf16[16,64,768]{2,1,0:T(8,128)(2,1)S(1)}, u32[]{:S(2)}, u32[]{:S(2)}) %all-to-all-start.1) | async-done | bytes 1572896 | tf_op jit(solution)/shard_map/all_to_all | solution.py:29
  121.7 1.4 copy-done.1
  123.2 1.4 copy-done.3
  124.6 4.2 %last.1 = (bf16[256,768]{1,0:T(8,128)(2,1)S(1)}, bf16[256,768]{1,0:T(8,128)(2,1)S(1)}, f32[776,768]{1,0:T(8,128)S(1)}, bf16[784,768]{1,0:T(8,128)(2,1)S(1)}) custom-call(f32[2]{0:T(128)S(1)} %pad_maximum_fusion.2.sb_ref, s32[1]{0:T(128)} %bitcast.core_ref, bf16[16,32,768]{2,1,0:T(8,128)(2,1)S(1)} %copy-done, ...), custom_call_target="tpu_custom_call" | custom-call | tf_op jit(solution)/shard_map/last/pallas_call | solution.py:262
  128.9 1.3 convolution_convert_fusion.1
  130.1 1.3 convolution_convert_fusion
  132.3 22.5 %all_to_all.30 = bf16[16,56,768]{2,1,0:T(8,128)(2,1)S(1)} all-to-all(bf16[16,56,768]{2,1,0:T(8,128)(2,1)S(1)} %pad_maximum_fusion), channel_id=1, replica_groups={{0,16,32,48,64,80,96,112,128,144,160,176,192,208,224,240},{1,17,33,49,6..., dimensions={0} | all-to-all | bytes 2752512 | tf_op jit(solution)/shard_map/all_to_all | solution.py:29
  155.4 13.1 %all_to_all.31 = bf16[8,8,768]{2,1,0:T(8,128)(2,1)S(1)} all-to-all(bf16[8,8,768]{2,1,0:T(8,128)(2,1)S(1)} %pad_maximum_fusion.1), channel_id=1, replica_groups={{0,2,4,6,8,10,12,14},{1,3,5,7,9,11,13,15},{16,18,20,22,24,26,28,30},{17..., dimensions={0} | all-to-all | bytes 196608 | tf_op jit(solution)/shard_map/all_to_all | solution.py:29
  168.6 10.0 %all_to_all.32 = bf16[8,6,768]{2,1,0:T(8,128)(2,1)S(1)} all-to-all(bf16[8,6,768]{2,1,0:T(8,128)(2,1)S(1)} %broadcast_in_dim.35), channel_id=1, replica_groups={{0,2,4,6,8,10,12,14},{1,3,5,7,9,11,13,15},{16,18,20,22,24,26,28,30},{17..., dimensions={0} | all-to-all | bytes 147456 | tf_op jit(solution)/shard_map/all_to_all | solution.py:29
  178.6 17.9 %all_to_all.33 = bf16[16,48,768]{2,1,0:T(8,128)(2,1)S(1)} all-to-all(bf16[16,48,768]{2,1,0:T(8,128)(2,1)S(1)} %broadcast_in_dim.37), channel_id=1, replica_groups={{0,16,32,48,64,80,96,112,128,144,160,176,192,208,224,240},{1,17,33,49,6..., dimensions={0} | all-to-all | bytes 2359296 | tf_op jit(solution)/shard_map/all_to_all | solution.py:29
  196.5 5.3 %collective-permute-start.63 = (bf16[768,768]{1,0:T(8,128)(2,1)S(1)}, bf16[768,768]{1,0:T(8,128)(2,1)S(1)}, u32[]{:S(2)}, u32[]{:S(2)}) collective-permute-start(bf16[768,768]{1,0:T(8,128)(2,1)S(1)} %bitcast.37), channel_id=1, source_target_pairs={{0,1},{1,0},{2,3},{3,2},{4,5},{5,4},{6,7},{7,6},{8,9},{9,8},{10,11... | collective-permute-start | bytes 3538952 | tf_op jit(solution)/shard_map/ppermute | solution.py:25
  202.5 1.5 write_head.2
  204.3 1.5 write_head.3
  (64 shorter events, 6.3 us)
Async XLA Ops:
  4.8 9.9 %copy-start.12 = (s32[4]{0:T(128)S(1)}, s32[4]{0:T(128)}, u32[]{:S(2)}) copy-start(s32[4]{0:T(128)} %param.49) | copy-start | bytes 52
  4.8 28.8 %collective-permute-start.61 = (bf16[16,32,768]{2,1,0:T(8,128)(2,1)}, bf16[16,32,768]{2,1,0:T(8,128)(2,1)S(1)}, u32[]{:S(2)}, u32[]{:S(2)}) collective-permute-start(bf16[16,32,768]{2,1,0:T(8,128)(2,1)} %get-tuple-element.244.both_ref), channel_id=1, source_target_pairs={{0,1},{1,2},{2,3},{3,4},{4,5},{5,6},{6,7},{7,8},{8,9},{9,10},{10,1... | collective-permute-start | bytes 2359304 | tf_op jit(solution)/shard_map/ppermute | solution.py:21
  7.9 25.7 %collective-permute-start.60 = (bf16[16,32,768]{2,1,0:T(8,128)(2,1)}, bf16[16,32,768]{2,1,0:T(8,128)(2,1)S(1)}, u32[]{:S(2)}, u32[]{:S(2)}) collective-permute-start(bf16[16,32,768]{2,1,0:T(8,128)(2,1)} %get-tuple-element.244.both_ref), channel_id=1, source_target_pairs={{0,255},{1,0},{2,1},{3,2},{4,3},{5,4},{6,5},{7,6},{8,7},{9,8},{10,... | collective-permute-start | bytes 2359304 | tf_op jit(solution)/shard_map/ppermute | solution.py:21
  8.2 25.4 %all-to-all-start = ((bf16[16,32,768]{2,1,0:T(8,128)(2,1)}), bf16[16,32,768]{2,1,0:T(8,128)(2,1)S(1)}, u32[]{:S(2)}, u32[]{:S(2)}) async-start(bf16[16,32,768]{2,1,0:T(8,128)(2,1)} %get-tuple-element.244.both_ref), calls=%async_computation | async-start | bytes 1572864 | tf_op jit(solution)/shard_map/all_to_all | solution.py:29
  33.6 0.9 copy-start.6
  33.6 1.1 copy-start.8
  34.7 23.2 %collective-permute-start.8 = (bf16[16,16,768]{2,1,0:T(8,128)(2,1)S(1)}, bf16[16,16,768]{2,1,0:T(8,128)(2,1)S(1)}, u32[]{:S(2)}, u32[]{:S(2)}) collective-permute-start(bf16[16,16,768]{2,1,0:T(8,128)(2,1)S(1)} %get-tuple-element.161), channel_id=1, source_target_pairs={{0,11},{1,12},{2,13},{3,14},{4,15},{5,0},{6,1},{7,2},{8,3},{9,4},{... | collective-permute-start | bytes 1179656 | tf_op jit(solution)/shard_map/cond/branch_5_fun/ppermute | solution.py:74
  36.1 24.5 %collective-permute-start.9 = (bf16[16,16,768]{2,1,0:T(8,128)(2,1)S(1)}, bf16[16,16,768]{2,1,0:T(8,128)(2,1)S(1)}, u32[]{:S(2)}, u32[]{:S(2)}) collective-permute-start(bf16[16,16,768]{2,1,0:T(8,128)(2,1)S(1)} %get-tuple-element.162), channel_id=1, source_target_pairs={{0,5},{1,6},{2,7},{3,8},{4,9},{5,10},{6,11},{7,12},{8,13},{9,14},{... | collective-permute-start | bytes 1179656 | tf_op jit(solution)/shard_map/cond/branch_5_fun/ppermute | solution.py:74
  74.7 13.6 %collective-permute-start.34 = (bf16[16,16,768]{2,1,0:T(8,128)(2,1)S(1)}, bf16[16,16,768]{2,1,0:T(8,128)(2,1)S(1)}, u32[]{:S(2)}, u32[]{:S(2)}) collective-permute-start(bf16[16,16,768]{2,1,0:T(8,128)(2,1)S(1)} %get-tuple-element.187), channel_id=1, source_target_pairs={{0,13},{1,14},{2,15},{3,0},{4,1},{5,2},{6,3},{7,4},{8,5},{9,6},{10... | collective-permute-start | bytes 1179656 | tf_op jit(solution)/shard_map/cond/branch_3_fun/ppermute | solution.py:74
  75.2 17.1 %collective-permute-start.35 = (bf16[16,16,768]{2,1,0:T(8,128)(2,1)S(1)}, bf16[16,16,768]{2,1,0:T(8,128)(2,1)S(1)}, u32[]{:S(2)}, u32[]{:S(2)}) collective-permute-start(bf16[16,16,768]{2,1,0:T(8,128)(2,1)S(1)} %get-tuple-element.188), channel_id=1, source_target_pairs={{0,3},{1,4},{2,5},{3,6},{4,7},{5,8},{6,9},{7,10},{8,11},{9,12},{10... | collective-permute-start | bytes 1179656 | tf_op jit(solution)/shard_map/cond/branch_3_fun/ppermute | solution.py:74
  94.5 6.7 %copy-start = (bf16[16,32,768]{2,1,0:T(8,128)(2,1)S(1)}, bf16[16,32,768]{2,1,0:T(8,128)(2,1)}, u32[]{:S(2)}) copy-start(bf16[16,32,768]{2,1,0:T(8,128)(2,1)} %get-tuple-element.244.both_ref) | copy-start | bytes 2359300
  94.5 27.2 %all-to-all-start.1 = ((bf16[16,64,768]{2,1,0:T(8,128)(2,1)}), bf16[16,64,768]{2,1,0:T(8,128)(2,1)S(1)}, u32[]{:S(2)}, u32[]{:S(2)}) async-start(bf16[16,64,768]{2,1,0:T(8,128)(2,1)} %line_up.1), calls=%async_computation.1 | async-start | bytes 3145728 | tf_op jit(solution)/shard_map/all_to_all | solution.py:29
  101.2 1.1 copy-start.7
  102.4 1.1 copy-start.9
  103.5 18.2 %copy-start.4 = (bf16[256,768]{1,0:T(8,128)(2,1)S(1)}, bf16[256,768]{1,0:T(8,128)(2,1)}, u32[]{:S(2)}) copy-start(bf16[256,768]{1,0:T(8,128)(2,1)} %xi_hbm.3) | copy-start | bytes 1179652
  103.5 18.2 %copy-start.5 = (bf16[256,768]{1,0:T(8,128)(2,1)S(1)}, bf16[256,768]{1,0:T(8,128)(2,1)}, u32[]{:S(2)}) copy-start(bf16[256,768]{1,0:T(8,128)(2,1)} %xt_hbm.3) | copy-start | bytes 1179652
  106.0 1.2 copy-start.2
  121.7 1.4 copy-start.1
  123.1 1.4 copy-start.3
  124.6 4.3 %copy-start.10 = (bf16[768,768]{1,0:T(8,128)(2,1)S(1)}, bf16[768,768]{1,0:T(8,128)(2,1)}, u32[]{:S(2)}) copy-start(bf16[768,768]{1,0:T(8,128)(2,1)} %wi_hbm.1) | copy-start | bytes 3538948
  128.7 1.4 copy-start.11
  128.8 3.0 %collective-permute-start.62 = (bf16[784,768]{1,0:T(8,128)(2,1)S(1)}, bf16[784,768]{1,0:T(8,128)(2,1)S(1)}, u32[]{:S(2)}, u32[]{:S(2)}) collective-permute-start(bf16[784,768]{1,0:T(8,128)(2,1)S(1)} %get-tuple-element.256), channel_id=1, source_target_pairs={{0,1},{1,0},{2,3},{3,2},{4,5},{5,4},{6,7},{7,6},{8,9},{9,8},{10,11... | collective-permute-start | bytes 3612680 | tf_op jit(solution)/shard_map/ppermute | solution.py:25
  196.5 7.8 %collective-permute-start.63 = (bf16[768,768]{1,0:T(8,128)(2,1)S(1)}, bf16[768,768]{1,0:T(8,128)(2,1)S(1)}, u32[]{:S(2)}, u32[]{:S(2)}) collective-permute-start(bf16[768,768]{1,0:T(8,128)(2,1)S(1)} %bitcast.37), channel_id=1, source_target_pairs={{0,1},{1,0},{2,3},{3,2},{4,5},{5,4},{6,7},{7,6},{8,9},{9,8},{10,11... | collective-permute-start | bytes 3538952 | tf_op jit(solution)/shard_map/ppermute | solution.py:25

commit v3 on v2

--- a/solution.py
+++ b/solution.py
@@ -203,12 +203,13 @@
     )(sb, *arrays)
 
 
-def last_kernel(sb_ref, core_ref, both_ref, far_ref, dz_ref, stats_ref, u_hbm, xi_hbm, xt_hbm,
-                dui_ref, dut_ref, kept_ref, given_ref, u_ref, x_ref, sems):
+def last_kernel(sb_ref, core_ref, both_ref, far_ref, stats_ref, dz_hbm, u_hbm, xi_hbm, xt_hbm,
+                dui_ref, dut_ref, kept_ref, given_ref, dz_ref, u_ref, x_ref, sems):
     copies = [
         pltpu.make_async_copy(u_hbm, u_ref, sems.at[0]),
         pltpu.make_async_copy(xi_hbm, x_ref.at[0], sems.at[1]),
         pltpu.make_async_copy(xt_hbm, x_ref.at[1], sems.at[2]),
+        pltpu.make_async_copy(dz_hbm, dz_ref, sems.at[3]),
     ]
     for copy in copies:
         copy.start()
@@ -217,6 +218,7 @@
     sums = tile_pair(sb_ref, zi, zt, piece_of(far_ref, 0, 4), piece_of(far_ref, 1, 4))
     sums = added(sums, tile_pair(sb_ref, zi, zt, piece_of(far_ref, 2, 4), piece_of(far_ref, 3, 4)))
     copies[0].wait()
+    copies[3].wait()
     for k, du_ref in enumerate((dui_ref, dut_ref)):
         dz = dz_ref[k] + sums[k]
         proj = u_ref[k * rows : (k + 1) * rows, :]
@@ -267,16 +269,17 @@
             jax.ShapeDtypeStruct((width + 8, width), jnp.float32),
             jax.ShapeDtypeStruct((width + 16, width), jnp.bfloat16),
         ),
-        in_specs=[pl.BlockSpec(memory_space=pltpu.SMEM)] * 2 + [vmem] * 4 + [pl.BlockSpec(memory_space=pl.ANY)] * 3,
+        in_specs=[pl.BlockSpec(memory_space=pltpu.SMEM)] * 2 + [vmem] * 3 + [pl.BlockSpec(memory_space=pl.ANY)] * 4,
         out_specs=(vmem,) * 4,
         scratch_shapes=[
+            pltpu.VMEM((2, rows, width), jnp.float32),
             pltpu.VMEM((2 * rows, width), jnp.float32),
             pltpu.VMEM((2, rows, width), jnp.bfloat16),
-            pltpu.SemaphoreType.DMA((3,)),
+            pltpu.SemaphoreType.DMA((4,)),
         ],
-        compiler_params=pltpu.CompilerParams(vmem_limit_bytes=40 * 1024 * 1024),
+        compiler_params=pltpu.CompilerParams(vmem_limit_bytes=49 * 1024 * 1024),
         name="last",
-    )(sb, core, both, far, dz, stats, u, image_feats, text_feats)
+    )(sb, core, both, far, stats, dz, u, image_feats, text_feats)
 
 
 def terms_of(stats):

time: 210 us -> 209 us (level); the launches traced: 206 us -> 209 us
  waiting for transfers between devices: 61.1 us -> 50.9 us
  loops' own time: 14.4 us -> 22 us
  starting transfers between devices: 27.5 us -> 33.6 us
  local copies, waits for them, and re-layouts: 8.51 us -> 5.66 us
  Pallas kernels: 15.7 us -> 18.1 us
    ppermute x4, waiting for transfers between devices: 36.5 us -> 27.9 us  [turned(): return lax.ppermute(value, 'pairs', pairs)]
    another operation x2, loops' own time: 14.4 us -> 22 us  [along(): return tuple(lax.switch(low, [branch(k) for k in range(STEP)], txt, img))]
    ppermute x2, starting transfers between devices: 5.42 us -> 9.54 us  [other_core(): lax.ppermute(value, 'pairs', [(source, source ^ 1) for source in range(CO...]
    all_to_all x2, starting transfers between devices: 11.7 us -> 14.7 us  [exchange(): lax.all_to_all(value, 'pairs', 0, 0, axis_index_groups=groups, tiled=True)]
    unnamed x26 -> x24, local copies, waits for them, and re-layouts: 7.36 us -> 4.51 us
    pallas_call x1, Pallas kernels: 4.18 us -> 6.63 us  [last(): pl.pallas_call(last_kernel, out_shape=(jax.ShapeDtypeStruct((rows, width)...]
  transfers between devices with their start and end apart: 10 -> 10, of which waited for: 8 -> 6; matrix products, arithmetic and copies ran while one was open for 2% -> 2% of each run, Pallas kernels for 2% -> 2%
where the time goes in v3:
time: 209 us
  blocking collectives  63 us (30%)
  waiting for transfers between devices  50.9 us (24%)
  starting transfers between devices  33.6 us (16%)
  loops' own time  22 us (11%)
  Pallas kernels  18.1 us (9%)
  between operations  10.4 us (5%)
  local copies, waits for them, and re-layouts  5.66 us (3%)
  matrix products  2.51 us (1%)
  other arithmetic  2.44 us (1%)
    all_to_all x4, blocking collectives, exchange(): lax.all_to_all(value, 'pairs', 0, 0, axis_index_groups=groups, tiled=True)  63 us
    ppermute x4, waiting for transfers between devices, turned(): return lax.ppermute(value, 'pairs', pairs)  27.9 us
    all_to_all x2, waiting for transfers between devices, exchange(): lax.all_to_all(value, 'pairs', 0, 0, axis_index_groups=groups, tiled=True)  22.7 us
    another operation x2, loops' own time, along(): return tuple(lax.switch(low, [branch(k) for k in range(STEP)], txt, img))  22 us
    all_to_all x2, starting transfers between devices, exchange(): lax.all_to_all(value, 'pairs', 0, 0, axis_index_groups=groups, tiled=True)  14.7 us
    ppermute x2, starting transfers between devices, other_core(): lax.ppermute(value, 'pairs', [(source, source ^ 1) for source in range(CO...  9.54 us
    pallas_call x1, Pallas kernels, last(): pl.pallas_call(last_kernel, out_shape=(jax.ShapeDtypeStruct((rows, width)...  6.63 us
    ppermute x4, starting transfers between devices, turned(): return lax.ppermute(value, 'pairs', pairs)  6.02 us
  transfers between devices with their start and end apart: 10, of which 6 were waited for; matrix products, arithmetic and copies ran while one was open for 2% of the time, Pallas kernels for 2%

profile of v3, /device:TPU:1, one launch (start us, length us, event | category | flops | bytes accessed | tf_op | source)
XLA Modules:
  0.0 208.6 jit_solution(11613883224582799218)
XLA Ops:
  0.6 4.1 %embed.1 = (bf16[16,32,768]{2,1,0:T(8,128)(2,1)}, f32[512,768]{1,0:T(8,128)}) custom-call(bf16[256,768]{1,0:T(8,128)(2,1)} %xi_hbm.3, bf16[256,768]{1,0:T(8,128)(2,1)} %xt_hbm.3, bf16[768,768]{1,0:T(8,128)(2,1)} %wi_hbm.1, bf16[768,768]{1,0:T(8,128)(2,1)} %wt_hbm.1), custom_call_target="tpu_custom_call" | custom-call | tf_op jit(solution)/shard_map/embed/pallas_call | solution.py:54
  4.8 3.1 %collective-permute-start.61 = (bf16[16,32,768]{2,1,0:T(8,128)(2,1)}, bf16[16,32,768]{2,1,0:T(8,128)(2,1)S(1)}, u32[]{:S(2)}, u32[]{:S(2)}) collective-permute-start(bf16[16,32,768]{2,1,0:T(8,128)(2,1)} %get-tuple-element.244.both_ref), channel_id=1, source_target_pairs={{0,1},{1,2},{2,3},{3,4},{4,5},{5,6},{6,7},{7,8},{8,9},{9,10},{10,1... | collective-permute-start | bytes 2359304 | tf_op jit(solution)/shard_map/ppermute | solution.py:21
  8.2 6.4 %all-to-all-start = ((bf16[16,32,768]{2,1,0:T(8,128)(2,1)}), bf16[16,32,768]{2,1,0:T(8,128)(2,1)S(1)}, u32[]{:S(2)}, u32[]{:S(2)}) async-start(bf16[16,32,768]{2,1,0:T(8,128)(2,1)} %get-tuple-element.244.both_ref), calls=%async_computation | async-start | bytes 1572864 | tf_op jit(solution)/shard_map/all_to_all | solution.py:29
  14.7 0.7 sort.15
  15.4 0.6 fusion.28
  24.1 9.5 %all-to-all-done = bf16[16,32,768]{2,1,0:T(8,128)(2,1)S(1)} async-done(((bf16[16,32,768]{2,1,0:T(8,128)(2,1)}), bf16[16,32,768]{2,1,0:T(8,128)(2,1)S(1)}, u32[]{:S(2)}, u32[]{:S(2)}) %all-to-all-start) | async-done | bytes 786464 | tf_op jit(solution)/shard_map/all_to_all | solution.py:29
  33.7 0.8 copy-done.4
  34.7 27.0 %conditional.2 = ((bf16[16,16,768]{2,1,0:T(8,128)(2,1)S(1)}, bf16[16,16,768]{2,1,0:T(8,128)(2,1)S(1)})) conditional(s32[]{:T(128)} %clamp.6, (bf16[16,16,768]{2,1,0:T(8,128)(2,1)S(1)}, bf16[16,16,768]{2,1,0:T(8,128)(2,1)S(1)}) %tuple.146, (bf16[16,16,768]{2,1,0:T(8,128)(2,1)S(1)}, ...), branch_computations={%region_1.2_spmd, %region_2.3_spmd, %region_3.4_spmd, %region_4.5_... | conditional | bytes 4718696 | solution.py:83
  34.7 2.4 %collective-permute-start.2 = (bf16[16,16,768]{2,1,0:T(8,128)(2,1)S(1)}, bf16[16,16,768]{2,1,0:T(8,128)(2,1)S(1)}, u32[]{:S(2)}, u32[]{:S(2)}) collective-permute-start(bf16[16,16,768]{2,1,0:T(8,128)(2,1)S(1)} %get-tuple-element.155), channel_id=1, source_target_pairs={{0,14},{1,15},{2,0},{3,1},{4,2},{5,3},{6,4},{7,5},{8,6},{9,7},{10,... | collective-permute-start | bytes 1179656 | tf_op jit(solution)/shard_map/cond/branch_2_fun/ppermute | solution.py:74
  37.1 7.6 %collective-permute-done.2 = bf16[16,16,768]{2,1,0:T(8,128)(2,1)S(1)} collective-permute-done((bf16[16,16,768]{2,1,0:T(8,128)(2,1)S(1)}, bf16[16,16,768]{2,1,0:T(8,128)(2,1)S(1)}, u32[]{:S(2)}, u32[]{:S(2)}) %collective-permute-start.2) | collective-permute-done | bytes 393248 | tf_op jit(solution)/shard_map/cond/branch_2_fun/ppermute | solution.py:74
  44.8 3.1 %collective-permute-done.3 = bf16[16,16,768]{2,1,0:T(8,128)(2,1)S(1)} collective-permute-done((bf16[16,16,768]{2,1,0:T(8,128)(2,1)S(1)}, bf16[16,16,768]{2,1,0:T(8,128)(2,1)S(1)}, u32[]{:S(2)}, u32[]{:S(2)}) %collective-permute-start.3) | collective-permute-done | bytes 393248 | tf_op jit(solution)/shard_map/cond/branch_2_fun/ppermute | solution.py:74
  61.9 28.9 %conditional.3 = ((bf16[16,16,768]{2,1,0:T(8,128)(2,1)S(1)}, bf16[16,16,768]{2,1,0:T(8,128)(2,1)S(1)})) conditional(s32[]{:T(128)} %clamp.7, (bf16[16,16,768]{2,1,0:T(8,128)(2,1)S(1)}, bf16[16,16,768]{2,1,0:T(8,128)(2,1)S(1)}) %tuple.147, (bf16[16,16,768]{2,1,0:T(8,128)(2,1)S(1)}, ...), branch_computations={%region_17.18_spmd, %region_18.19_spmd, %region_19.20_spmd, %regio... | conditional | bytes 4718696 | solution.py:83
  70.0 3.6 %collective-permute-start.53 = (bf16[16,16,768]{2,1,0:T(8,128)(2,1)S(1)}, bf16[16,16,768]{2,1,0:T(8,128)(2,1)S(1)}, u32[]{:S(2)}, u32[]{:S(2)}) collective-permute-start(bf16[16,16,768]{2,1,0:T(8,128)(2,1)S(1)} %get-tuple-element.206), channel_id=1, source_target_pairs={{0,12},{1,13},{2,14},{3,15},{4,0},{5,1},{6,2},{7,3},{8,4},{9,5},{1... | collective-permute-start | bytes 1179656 | tf_op jit(solution)/shard_map/cond/branch_12_fun/ppermute | solution.py:74
  73.5 17.2 %collective-permute-done.52 = bf16[16,16,768]{2,1,0:T(8,128)(2,1)S(1)} collective-permute-done((bf16[16,16,768]{2,1,0:T(8,128)(2,1)S(1)}, bf16[16,16,768]{2,1,0:T(8,128)(2,1)S(1)}, u32[]{:S(2)}, u32[]{:S(2)}) %collective-permute-start.52) | collective-permute-done | bytes 393248 | tf_op jit(solution)/shard_map/cond/branch_12_fun/ppermute | solution.py:74
  90.8 1.8 line_up.1
  92.6 8.2 %all-to-all-start.1 = ((bf16[16,64,768]{2,1,0:T(8,128)(2,1)}), bf16[16,64,768]{2,1,0:T(8,128)(2,1)S(1)}, u32[]{:S(2)}, u32[]{:S(2)}) async-start(bf16[16,64,768]{2,1,0:T(8,128)(2,1)} %line_up.1), calls=%async_computation.1 | async-start | bytes 3145728 | tf_op jit(solution)/shard_map/all_to_all | solution.py:29
  102.2 1.1 copy-done.5
  103.4 1.1 copy-done.7
  104.5 2.5 %near.1 = (f32[2,256,768]{2,1,0:T(8,128)S(1)}, f32[3,8,256]{2,1,0:T(8,128)S(1)}) custom-call(f32[2]{0:T(128)S(1)} %pad_maximum_fusion.2.sb_ref, bf16[16,32,768]{2,1,0:T(8,128)(2,1)S(1)} %copy-done, bf16[16,32,768]{2,1,0:T(8,128)(2,1)S(1)} %copy-done.7, bf16[16,32,768]{2,1,0:T(8,128)(2,1)S(1)} %copy-done.5), custom_call_target="tpu_custom_call" | custom-call | flops 1509949440 | bytes 3145728 | tf_op jit(solution)/shard_map/near/pallas_call | solution.py:192
  107.1 1.2 copy-done.1
  108.2 13.2 %all-to-all-done.1.far_ref = bf16[16,64,768]{2,1,0:T(8,128)(2,1)S(1)} async-done(((bf16[16,64,768]{2,1,0:T(8,128)(2,1)}), bf16[16,64,768]{2,1,0:T(8,128)(2,1)S(1)}, u32[]{:S(2)}, u32[]{:S(2)}) %all-to-all-start.1) | async-done | bytes 1572896 | tf_op jit(solution)/shard_map/all_to_all | solution.py:29
  121.4 6.6 %last.1 = (bf16[256,768]{1,0:T(8,128)(2,1)S(1)}, bf16[256,768]{1,0:T(8,128)(2,1)S(1)}, f32[776,768]{1,0:T(8,128)}, bf16[784,768]{1,0:T(8,128)(2,1)S(1)}) custom-call(f32[2]{0:T(128)S(1)} %pad_maximum_fusion.2.sb_ref, s32[1]{0:T(128)} %bitcast.core_ref, bf16[16,32,768]{2,1,0:T(8,128)(2,1)S(1)} %copy-done, bf16[16,64,768]{2,1,0:T(8,128)(2,1)S(1)} %all-to-all-done.1.far_ref, ...), custom_call_target="tpu_custom_call" | custom-call | tf_op jit(solution)/shard_map/last/pallas_call | solution.py:264
  128.1 4.2 %collective-permute-start.62 = (bf16[784,768]{1,0:T(8,128)(2,1)S(1)}, bf16[784,768]{1,0:T(8,128)(2,1)S(1)}, u32[]{:S(2)}, u32[]{:S(2)}) collective-permute-start(bf16[784,768]{1,0:T(8,128)(2,1)S(1)} %get-tuple-element.256), channel_id=1, source_target_pairs={{0,1},{1,0},{2,3},{3,2},{4,5},{5,4},{6,7},{7,6},{8,9},{9,8},{10,11... | collective-permute-start | bytes 3612680 | tf_op jit(solution)/shard_map/ppermute | solution.py:25
  132.3 1.3 convolution_convert_fusion.1
  133.6 1.3 convolution_convert_fusion
  135.4 22.7 %all_to_all.30 = bf16[16,56,768]{2,1,0:T(8,128)(2,1)S(1)} all-to-all(bf16[16,56,768]{2,1,0:T(8,128)(2,1)S(1)} %pad_maximum_fusion), channel_id=1, replica_groups={{0,16,32,48,64,80,96,112,128,144,160,176,192,208,224,240},{1,17,33,49,6..., dimensions={0} | all-to-all | bytes 2752512 | tf_op jit(solution)/shard_map/all_to_all | solution.py:29
  158.7 12.4 %all_to_all.31 = bf16[8,8,768]{2,1,0:T(8,128)(2,1)S(1)} all-to-all(bf16[8,8,768]{2,1,0:T(8,128)(2,1)S(1)} %pad_maximum_fusion.1), channel_id=1, replica_groups={{0,2,4,6,8,10,12,14},{1,3,5,7,9,11,13,15},{16,18,20,22,24,26,28,30},{17..., dimensions={0} | all-to-all | bytes 196608 | tf_op jit(solution)/shard_map/all_to_all | solution.py:29
  171.2 10.0 %all_to_all.32 = bf16[8,6,768]{2,1,0:T(8,128)(2,1)S(1)} all-to-all(bf16[8,6,768]{2,1,0:T(8,128)(2,1)S(1)} %broadcast_in_dim.35), channel_id=1, replica_groups={{0,2,4,6,8,10,12,14},{1,3,5,7,9,11,13,15},{16,18,20,22,24,26,28,30},{17..., dimensions={0} | all-to-all | bytes 147456 | tf_op jit(solution)/shard_map/all_to_all | solution.py:29
  181.2 17.9 %all_to_all.33 = bf16[16,48,768]{2,1,0:T(8,128)(2,1)S(1)} all-to-all(bf16[16,48,768]{2,1,0:T(8,128)(2,1)S(1)} %broadcast_in_dim.37), channel_id=1, replica_groups={{0,16,32,48,64,80,96,112,128,144,160,176,192,208,224,240},{1,17,33,49,6..., dimensions={0} | all-to-all | bytes 2359296 | tf_op jit(solution)/shard_map/all_to_all | solution.py:29
  199.1 5.3 %collective-permute-start.63 = (bf16[768,768]{1,0:T(8,128)(2,1)S(1)}, bf16[768,768]{1,0:T(8,128)(2,1)S(1)}, u32[]{:S(2)}, u32[]{:S(2)}) collective-permute-start(bf16[768,768]{1,0:T(8,128)(2,1)S(1)} %bitcast.37), channel_id=1, source_target_pairs={{0,1},{1,0},{2,3},{3,2},{4,5},{5,4},{6,7},{7,6},{8,9},{9,8},{10,11... | collective-permute-start | bytes 3538952 | tf_op jit(solution)/shard_map/ppermute | solution.py:25
  205.1 1.5 write_head.2
  206.9 1.5 write_head.3
  (62 shorter events, 3.3 us)
Async XLA Ops:
  4.8 9.9 %copy-start.11 = (s32[4]{0:T(128)S(1)}, s32[4]{0:T(128)}, u32[]{:S(2)}) copy-start(s32[4]{0:T(128)} %param.49) | copy-start | bytes 52
  4.8 28.8 %collective-permute-start.61 = (bf16[16,32,768]{2,1,0:T(8,128)(2,1)}, bf16[16,32,768]{2,1,0:T(8,128)(2,1)S(1)}, u32[]{:S(2)}, u32[]{:S(2)}) collective-permute-start(bf16[16,32,768]{2,1,0:T(8,128)(2,1)} %get-tuple-element.244.both_ref), channel_id=1, source_target_pairs={{0,1},{1,2},{2,3},{3,4},{4,5},{5,6},{6,7},{7,8},{8,9},{9,10},{10,1... | collective-permute-start | bytes 2359304 | tf_op jit(solution)/shard_map/ppermute | solution.py:21
  7.9 25.7 %collective-permute-start.60 = (bf16[16,32,768]{2,1,0:T(8,128)(2,1)}, bf16[16,32,768]{2,1,0:T(8,128)(2,1)S(1)}, u32[]{:S(2)}, u32[]{:S(2)}) collective-permute-start(bf16[16,32,768]{2,1,0:T(8,128)(2,1)} %get-tuple-element.244.both_ref), channel_id=1, source_target_pairs={{0,255},{1,0},{2,1},{3,2},{4,3},{5,4},{6,5},{7,6},{8,7},{9,8},{10,... | collective-permute-start | bytes 2359304 | tf_op jit(solution)/shard_map/ppermute | solution.py:21
  8.2 25.4 %all-to-all-start = ((bf16[16,32,768]{2,1,0:T(8,128)(2,1)}), bf16[16,32,768]{2,1,0:T(8,128)(2,1)S(1)}, u32[]{:S(2)}, u32[]{:S(2)}) async-start(bf16[16,32,768]{2,1,0:T(8,128)(2,1)} %get-tuple-element.244.both_ref), calls=%async_computation | async-start | bytes 1572864 | tf_op jit(solution)/shard_map/all_to_all | solution.py:29
  33.6 0.9 copy-start.4
  33.6 1.1 copy-start.6
  34.7 10.0 %collective-permute-start.2 = (bf16[16,16,768]{2,1,0:T(8,128)(2,1)S(1)}, bf16[16,16,768]{2,1,0:T(8,128)(2,1)S(1)}, u32[]{:S(2)}, u32[]{:S(2)}) collective-permute-start(bf16[16,16,768]{2,1,0:T(8,128)(2,1)S(1)} %get-tuple-element.155), channel_id=1, source_target_pairs={{0,14},{1,15},{2,0},{3,1},{4,2},{5,3},{6,4},{7,5},{8,6},{9,7},{10,... | collective-permute-start | bytes 1179656 | tf_op jit(solution)/shard_map/cond/branch_2_fun/ppermute | solution.py:74
  37.1 10.7 %collective-permute-start.3 = (bf16[16,16,768]{2,1,0:T(8,128)(2,1)S(1)}, bf16[16,16,768]{2,1,0:T(8,128)(2,1)S(1)}, u32[]{:S(2)}, u32[]{:S(2)}) collective-permute-start(bf16[16,16,768]{2,1,0:T(8,128)(2,1)S(1)} %get-tuple-element.156), channel_id=1, source_target_pairs={{0,2},{1,3},{2,4},{3,5},{4,6},{5,7},{6,8},{7,9},{8,10},{9,11},{10,... | collective-permute-start | bytes 1179656 | tf_op jit(solution)/shard_map/cond/branch_2_fun/ppermute | solution.py:74
  69.9 20.8 %collective-permute-start.52 = (bf16[16,16,768]{2,1,0:T(8,128)(2,1)S(1)}, bf16[16,16,768]{2,1,0:T(8,128)(2,1)S(1)}, u32[]{:S(2)}, u32[]{:S(2)}) collective-permute-start(bf16[16,16,768]{2,1,0:T(8,128)(2,1)S(1)} %get-tuple-element.205), channel_id=1, source_target_pairs={{0,4},{1,5},{2,6},{3,7},{4,8},{5,9},{6,10},{7,11},{8,12},{9,13},{1... | collective-permute-start | bytes 1179656 | tf_op jit(solution)/shard_map/cond/branch_12_fun/ppermute | solution.py:74
  70.0 20.8 %collective-permute-start.53 = (bf16[16,16,768]{2,1,0:T(8,128)(2,1)S(1)}, bf16[16,16,768]{2,1,0:T(8,128)(2,1)S(1)}, u32[]{:S(2)}, u32[]{:S(2)}) collective-permute-start(bf16[16,16,768]{2,1,0:T(8,128)(2,1)S(1)} %get-tuple-element.206), channel_id=1, source_target_pairs={{0,12},{1,13},{2,14},{3,15},{4,0},{5,1},{6,2},{7,3},{8,4},{9,5},{1... | collective-permute-start | bytes 1179656 | tf_op jit(solution)/shard_map/cond/branch_12_fun/ppermute | solution.py:74
  92.6 9.6 %copy-start = (bf16[16,32,768]{2,1,0:T(8,128)(2,1)S(1)}, bf16[16,32,768]{2,1,0:T(8,128)(2,1)}, u32[]{:S(2)}) copy-start(bf16[16,32,768]{2,1,0:T(8,128)(2,1)} %get-tuple-element.244.both_ref) | copy-start | bytes 2359300
  92.6 28.8 %all-to-all-start.1 = ((bf16[16,64,768]{2,1,0:T(8,128)(2,1)}), bf16[16,64,768]{2,1,0:T(8,128)(2,1)S(1)}, u32[]{:S(2)}, u32[]{:S(2)}) async-start(bf16[16,64,768]{2,1,0:T(8,128)(2,1)} %line_up.1), calls=%async_computation.1 | async-start | bytes 3145728 | tf_op jit(solution)/shard_map/all_to_all | solution.py:29
  102.2 1.1 copy-start.5
  103.4 1.1 copy-start.7
  104.5 16.9 %copy-start.2 = (bf16[256,768]{1,0:T(8,128)(2,1)S(1)}, bf16[256,768]{1,0:T(8,128)(2,1)}, u32[]{:S(2)}) copy-start(bf16[256,768]{1,0:T(8,128)(2,1)} %xi_hbm.3) | copy-start | bytes 1179652
  104.5 16.9 %copy-start.3 = (bf16[256,768]{1,0:T(8,128)(2,1)S(1)}, bf16[256,768]{1,0:T(8,128)(2,1)}, u32[]{:S(2)}) copy-start(bf16[256,768]{1,0:T(8,128)(2,1)} %xt_hbm.3) | copy-start | bytes 1179652
  107.1 1.2 copy-start.1
  121.4 10.9 %copy-start.8 = (bf16[768,768]{1,0:T(8,128)(2,1)S(1)}, bf16[768,768]{1,0:T(8,128)(2,1)}, u32[]{:S(2)}) copy-start(bf16[768,768]{1,0:T(8,128)(2,1)} %wi_hbm.1) | copy-start | bytes 3538948
  128.1 5.5 %copy-start.9 = (bf16[768,768]{1,0:T(8,128)(2,1)S(1)}, bf16[768,768]{1,0:T(8,128)(2,1)}, u32[]{:S(2)}) copy-start(bf16[768,768]{1,0:T(8,128)(2,1)} %wt_hbm.1) | copy-start | bytes 3538948
  128.1 6.7 %collective-permute-start.62 = (bf16[784,768]{1,0:T(8,128)(2,1)S(1)}, bf16[784,768]{1,0:T(8,128)(2,1)S(1)}, u32[]{:S(2)}, u32[]{:S(2)}) collective-permute-start(bf16[784,768]{1,0:T(8,128)(2,1)S(1)} %get-tuple-element.256), channel_id=1, source_target_pairs={{0,1},{1,0},{2,3},{3,2},{4,5},{5,4},{6,7},{7,6},{8,9},{9,8},{10,11... | collective-permute-start | bytes 3612680 | tf_op jit(solution)/shard_map/ppermute | solution.py:25
  132.3 2.5 %copy-start.10 = (f32[776,768]{1,0:T(8,128)S(1)}, f32[776,768]{1,0:T(8,128)}, u32[]{:S(2)}) copy-start(f32[776,768]{1,0:T(8,128)} %get-tuple-element.261) | copy-start | bytes 7151620
  199.1 7.8 %collective-permute-start.63 = (bf16[768,768]{1,0:T(8,128)(2,1)S(1)}, bf16[768,768]{1,0:T(8,128)(2,1)S(1)}, u32[]{:S(2)}, u32[]{:S(2)}) collective-permute-start(bf16[768,768]{1,0:T(8,128)(2,1)S(1)} %bitcast.37), channel_id=1, source_target_pairs={{0,1},{1,0},{2,3},{3,2},{4,5},{5,4},{6,7},{7,6},{8,9},{9,8},{10,11... | collective-permute-start | bytes 3538952 | tf_op jit(solution)/shard_map/ppermute | solution.py:25
